TPU v7x, 32 devices: a whole 2x2x4 slice. The times are simulated.
32 devices in a mesh: batch: 8 (over z, y), rows: 4 (over x, core).
Axes of the slice: x: 2, y: 2, z: 4, core: 2. Of those that a mesh axis runs over, the one named last changes fastest.
Arguments:
- large_in: bfloat16 [192, 4, 4, 14, 384], P('batch', 'rows'), may hold values from -6 to 6
- small_in: bfloat16 [576, 4, 2, 6, 384], P('batch', 'rows'), may hold values from -6 to 6
- large_cot: bfloat16 [192, 4, 4, 14, 384], P('batch', 'rows'), may hold values from -6 to 6
- small_cot: bfloat16 [576, 4, 2, 6, 384], P('batch', 'rows'), may hold values from -6 to 6
- crop_counts: int32 [8, 2], P('batch'), may hold values from 12 to 72, as said below
- band_bounds: int32 [2, 5], replicated, may hold values from 0 to 14, as said below
- row_interp: float32 [6, 14], replicated, may hold values from 0 to 0.5
- col_interp: float32 [4, 8], replicated, may hold values from 0 to 0.5
- norm1_gain: float32 [2, 384], replicated, may hold values from 0.5 to 1.5
- norm1_bias: float32 [2, 384], replicated, may hold values from -2 to 2
- filters: float32 [2, 2, 14, 8, 384], replicated, may hold values from -4 to 4
- norm2_gain: float32 [2, 384], replicated, may hold values from 0.5 to 1.5
- norm2_bias: float32 [2, 384], replicated, may hold values from -2 to 2
- fc1_weight: bfloat16 [2, 384, 1536], replicated, may hold values from -0.3125 to 0.3125
- fc1_bias: float32 [2, 1536], replicated, may hold values from -2 to 2
- fc2_weight: bfloat16 [2, 1536, 384], replicated, may hold values from -0.15625 to 0.15625
- fc2_bias: float32 [2, 384], replicated, may hold values from -2 to 2
Outputs:
- large_out: float32 [192, 4, 4, 14, 384], P('batch', 'rows')
- small_out: float32 [576, 4, 2, 6, 384], P('batch', 'rows')
- large_grad: float32 [192, 4, 4, 14, 384], P('batch', 'rows')
- small_grad: float32 [576, 4, 2, 6, 384], P('batch', 'rows')
- grad_norm1_gain: float32 [2, 384], replicated
- grad_norm1_bias: float32 [2, 384], replicated
- grad_filters: float32 [2, 2, 14, 8, 384], replicated
- grad_norm2_gain: float32 [2, 384], replicated
- grad_norm2_bias: float32 [2, 384], replicated
- grad_fc1_weight: float32 [2, 384, 1536], replicated
- grad_fc1_bias: float32 [2, 1536], replicated
- grad_fc2_weight: float32 [2, 1536, 384], replicated
- grad_fc2_bias: float32 [2, 384], replicated
Inputs may be any that keep to these rules, and one draw needn't show every extreme that they name: `crop_counts`: row b gives the live large and live small crops on each device of batch index b: at least half of 24 and of 72; in every draw some batch index has all 24 and 72 live. `band_bounds`: row 0 cuts the 14 rows of a large crop into one band per rows index, row 1 the 6 rows of a small crop: entry j is band j's first row, the last entry is the grid's height. Large bands hold 1 to 4 rows, small ones 0 to 2, and in each row some band holds exactly its most.
All inputs are finite; a program needn't handle non-finite values.
Results may differ from a plain program's by a relative error of at most 0.025.
The roundings to bfloat16 on the way count: a program that leaves them out, or rounds other values in their place, can miss the bound.
Values may be sent and summed in bfloat16 or wider, within the bound.
A program may use at most 256 MiB of HBM per device.

v0:
```python
from functools import partial
import math

import jax
import jax.numpy as jnp
from jax import lax
from jax.sharding import PartitionSpec as P

HL = 14
WL = 14
FL = 8
HS = 6
WS = 6
FS = 4
BL = 4
BS = 2
KL = 16
KS = 8
LAYERS = 2


EPSILON = 1e-06
HIGHEST = lax.Precision.HIGHEST


def spectral_tables(first_row, band_rows, grid_height, grid_width, col_count, padded, slot_count):
    row_freq = jnp.arange(padded, dtype=jnp.int32)[:, None, None, None]
    col_freq = jnp.arange(col_count, dtype=jnp.int32)[None, :, None, None]
    slot_ids = jnp.arange(slot_count, dtype=jnp.int32)[None, None, :, None]
    columns = jnp.arange(grid_width, dtype=jnp.int32)[None, None, None, :]
    phase = (row_freq * (first_row + slot_ids) * grid_width + col_freq * columns * grid_height) % (
        grid_height * grid_width
    )
    angle = phase.astype(jnp.float32) * jnp.float32(2.0 * math.pi / (grid_height * grid_width))
    inside = ((row_freq < grid_height) & (slot_ids < band_rows)).astype(jnp.float32) * jnp.float32(
        1.0 / math.sqrt(grid_height * grid_width)
    )
    forward = jnp.stack([jnp.cos(angle) * inside, -jnp.sin(angle) * inside])
    folding = jnp.where((col_freq == 0) | (2 * col_freq == grid_width), 1.0, 2.0).astype(
        jnp.float32
    )
    return (forward.astype(jnp.bfloat16), (forward * folding).astype(jnp.bfloat16))


def layer_norm(values, norm_gain, norm_bias):
    centred = values - jnp.mean(values, axis=-1, keepdims=True)
    variance = jnp.mean(centred * centred, axis=-1, keepdims=True)
    return centred * lax.rsqrt(variance + EPSILON) * norm_gain + norm_bias


def transform(table, values):
    return jnp.einsum("cjklsw,iswd->icjkld", table, values, preferred_element_type=jnp.float32)


def untransform(table, spectrum):
    return jnp.einsum("cjklsw,icjkld->iswd", table, spectrum, preferred_element_type=jnp.float32)


def apply_filter(spectrum, used_filter):
    real_part = spectrum[:, 0] * used_filter[0] - spectrum[:, 1] * used_filter[1]
    imag_part = spectrum[:, 0] * used_filter[1] + spectrum[:, 1] * used_filter[0]
    return jnp.stack([real_part, imag_part], axis=1)


def filter_back(grad_spec, spectrum, used_filter):
    grad_real = grad_spec[:, 0]
    grad_imag = grad_spec[:, 1]
    grad_input = jnp.stack(
        [
            grad_real * used_filter[0] + grad_imag * used_filter[1],
            grad_imag * used_filter[0] - grad_real * used_filter[1],
        ],
        axis=1,
    )
    grad_filter = jnp.stack(
        [
            jnp.sum(grad_real * spectrum[:, 0] + grad_imag * spectrum[:, 1], axis=0),
            jnp.sum(grad_imag * spectrum[:, 0] - grad_real * spectrum[:, 1], axis=0),
        ]
    )
    return (grad_input, grad_filter)


def pad_rows(spectral_filter, padded):
    return jnp.pad(
        spectral_filter, ((0, 0), (0, padded - spectral_filter.shape[1]), (0, 0), (0, 0))
    )


def owned_rows(padded_filter, row_count, row_place):
    whole = padded_filter.reshape(
        (2, row_count, padded_filter.shape[1] // row_count) + padded_filter.shape[2:]
    )
    return lax.dynamic_slice_in_dim(whole, row_place, 1, axis=1)


def placed_rows(grad_filter, padded, height_used, row_count, row_place):
    whole = jnp.zeros((2, row_count) + grad_filter.shape[2:], jnp.float32)
    whole = lax.dynamic_update_slice_in_dim(whole, grad_filter, row_place, axis=1)
    return whole.reshape((2, padded) + grad_filter.shape[3:])[:, :height_used]


def local(
    large_in,
    small_in,
    large_cot,
    small_cot,
    crop_counts,
    band_bounds,
    row_interp,
    col_interp,
    norm1_gain,
    norm1_bias,
    filters,
    norm2_gain,
    norm2_bias,
    fc1_weight,
    fc1_bias,
    fc2_weight,
    fc2_bias,
):
    row_count = lax.axis_size("rows")
    row_place = lax.axis_index("rows")
    heights = (HL, HS)
    grid_widths = (WL, WS)
    col_counts = (FL, FS)
    paddings = (KL, KS)
    slot_counts = (BL, BS)
    crops_in = (large_in, small_in)
    crops_cot = (large_cot, small_cot)
    own_forward = []
    own_inverse = []
    full_forward = []
    full_inverse = []
    masks = []
    values = []
    grads = []
    for crop_kind in range(2):
        first_row = band_bounds[crop_kind, row_place]
        band_rows = band_bounds[crop_kind, row_place + 1] - first_row
        table_shape = (
            2,
            row_count,
            paddings[crop_kind] // row_count,
            col_counts[crop_kind],
            slot_counts[crop_kind],
            grid_widths[crop_kind],
        )
        forward, inverse = spectral_tables(
            first_row,
            band_rows,
            heights[crop_kind],
            grid_widths[crop_kind],
            col_counts[crop_kind],
            paddings[crop_kind],
            slot_counts[crop_kind],
        )
        own_forward.append(forward.reshape(table_shape))
        own_inverse.append(inverse.reshape(table_shape))
        all_first = band_bounds[crop_kind, :-1]
        all_rows = band_bounds[crop_kind, 1:] - all_first
        every_forward, every_inverse = jax.vmap(
            lambda start_row, rows_in: spectral_tables(
                start_row,
                rows_in,
                heights[crop_kind],
                grid_widths[crop_kind],
                col_counts[crop_kind],
                paddings[crop_kind],
                slot_counts[crop_kind],
            )
        )(all_first, all_rows)
        full_forward.append(every_forward)
        full_inverse.append(every_inverse)
        live_crops = (
            jnp.arange(crops_in[crop_kind].shape[0], dtype=jnp.int32) < crop_counts[0, crop_kind]
        )
        live_slots = jnp.arange(slot_counts[crop_kind], dtype=jnp.int32) < band_rows
        masks.append(
            (live_crops[:, None] & live_slots[None, :]).astype(jnp.float32)[:, :, None, None]
        )
        values.append(crops_in[crop_kind][:, 0].astype(jnp.float32))
        grads.append(crops_cot[crop_kind][:, 0].astype(jnp.float32) * masks[crop_kind])
    records = []
    for layer_index in range(LAYERS):
        small_filter = jnp.einsum(
            "ka,cabd,lb->ckld", row_interp, filters[layer_index], col_interp, precision=HIGHEST
        )
        padded_filters = (pad_rows(filters[layer_index], KL), pad_rows(small_filter, KS))
        norm_backs = []
        normed_all = []
        for crop_kind in range(2):
            normed, norm_back = jax.vjp(
                layer_norm, values[crop_kind], norm1_gain[layer_index], norm1_bias[layer_index]
            )
            norm_backs.append(norm_back)
            normed_all.append(normed)
        used_filters = (
            owned_rows(padded_filters[0], row_count, row_place),
            owned_rows(padded_filters[1], row_count, row_place),
        )
        band_parts = [
            transform(own_forward[crop_kind], normed_all[crop_kind].astype(jnp.bfloat16))
            for crop_kind in range(2)
        ]
        spectra = (
            lax.psum_scatter(
                band_parts[0].astype(jnp.bfloat16), "rows", scatter_dimension=2, tiled=True
            ).astype(jnp.float32),
            lax.psum_scatter(
                band_parts[1].astype(jnp.bfloat16), "rows", scatter_dimension=2, tiled=True
            ).astype(jnp.float32),
        )
        filtered = [
            apply_filter(spectra[crop_kind], used_filters[crop_kind]).astype(jnp.bfloat16)
            for crop_kind in range(2)
        ]

        def inverse_add(pieces):
            return tuple((untransform(own_inverse[member], pieces[member]) for member in range(2)))

        mixed = inverse_add(
            (
                lax.all_gather(filtered[0], "rows", axis=2, tiled=True),
                lax.all_gather(filtered[1], "rows", axis=2, tiled=True),
            )
        )
        layer_record = []
        next_values = []
        for crop_kind in range(2):
            second, second_back = jax.vjp(
                layer_norm, mixed[crop_kind], norm2_gain[layer_index], norm2_bias[layer_index]
            )
            second_flat = second.reshape(-1, second.shape[-1]).astype(jnp.bfloat16)
            hidden = (
                jnp.dot(second_flat, fc1_weight[layer_index], preferred_element_type=jnp.float32)
                + fc1_bias[layer_index]
            )
            active = jax.nn.gelu(hidden, approximate=False).astype(jnp.bfloat16)
            branch = (
                jnp.dot(active, fc2_weight[layer_index], preferred_element_type=jnp.float32)
                + fc2_bias[layer_index]
            )
            layer_record.append(
                (
                    norm_backs[crop_kind],
                    spectra[crop_kind],
                    second_back,
                    second_flat,
                    hidden,
                    active,
                )
            )
            next_values.append(values[crop_kind] + branch.reshape(values[crop_kind].shape))
        records.append((used_filters, layer_record))
        values = next_values
    layer_grads = [None] * LAYERS
    for layer_index in reversed(range(LAYERS)):
        used_filters, layer_record = records[layer_index]
        grad_weight_two = jnp.zeros(fc2_weight.shape[1:], jnp.float32)
        grad_bias_out = jnp.zeros(fc2_bias.shape[1:], jnp.float32)
        grad_weight_one = jnp.zeros(fc1_weight.shape[1:], jnp.float32)
        grad_bias_hidden = jnp.zeros(fc1_bias.shape[1:], jnp.float32)
        grad_gain_two = jnp.zeros(norm2_gain.shape[1:], jnp.float32)
        grad_bias_two = jnp.zeros(norm2_bias.shape[1:], jnp.float32)
        grad_gain_one = jnp.zeros(norm1_gain.shape[1:], jnp.float32)
        grad_bias_one = jnp.zeros(norm1_bias.shape[1:], jnp.float32)
        mixed_grads = []
        for crop_kind in range(2):
            norm_back, spectrum, second_back, second_flat, hidden, active = layer_record[crop_kind]
            out_grad = grads[crop_kind].reshape(-1, grads[crop_kind].shape[-1]).astype(jnp.bfloat16)
            grad_weight_two = grad_weight_two + jnp.einsum(
                "nf,nd->fd", active, out_grad, preferred_element_type=jnp.float32
            )
            grad_bias_out = grad_bias_out + jnp.sum(out_grad.astype(jnp.float32), axis=0)
            active_grad = jnp.dot(
                out_grad, fc2_weight[layer_index].T, preferred_element_type=jnp.float32
            )
            hidden_grad = jax.vjp(partial(jax.nn.gelu, approximate=False), hidden)[1](active_grad)[
                0
            ].astype(jnp.bfloat16)
            grad_weight_one = grad_weight_one + jnp.einsum(
                "nd,nf->df", second_flat, hidden_grad, preferred_element_type=jnp.float32
            )
            grad_bias_hidden = grad_bias_hidden + jnp.sum(hidden_grad.astype(jnp.float32), axis=0)
            second_grad = jnp.dot(
                hidden_grad, fc1_weight[layer_index].T, preferred_element_type=jnp.float32
            ).reshape(grads[crop_kind].shape)
            mixed_grad, gain_part, bias_part = second_back(second_grad)
            grad_gain_two = grad_gain_two + gain_part
            grad_bias_two = grad_bias_two + bias_part
            mixed_grads.append(mixed_grad)
        band_grads = [
            transform(own_inverse[crop_kind], mixed_grads[crop_kind].astype(jnp.bfloat16))
            for crop_kind in range(2)
        ]
        spectrum_grads = (
            lax.psum_scatter(
                band_grads[0].astype(jnp.bfloat16), "rows", scatter_dimension=2, tiled=True
            ).astype(jnp.float32),
            lax.psum_scatter(
                band_grads[1].astype(jnp.bfloat16), "rows", scatter_dimension=2, tiled=True
            ).astype(jnp.float32),
        )
        filter_parts = []
        sent = []
        for crop_kind in range(2):
            input_grad, filter_grad = filter_back(
                spectrum_grads[crop_kind], layer_record[crop_kind][1], used_filters[crop_kind]
            )
            filter_parts.append(
                placed_rows(
                    filter_grad, paddings[crop_kind], heights[crop_kind], row_count, row_place
                )
            )
            sent.append(input_grad.astype(jnp.bfloat16))

        def forward_add(pieces):
            return tuple((untransform(own_forward[member], pieces[member]) for member in range(2)))

        normed_grads = forward_add(
            (
                lax.all_gather(sent[0], "rows", axis=2, tiled=True),
                lax.all_gather(sent[1], "rows", axis=2, tiled=True),
            )
        )
        grad_filter = filter_parts[0] + jnp.einsum(
            "ka,ckld,lb->cabd", row_interp, filter_parts[1], col_interp, precision=HIGHEST
        )
        for crop_kind in range(2):
            value_grad, gain_part, bias_part = layer_record[crop_kind][0](normed_grads[crop_kind])
            grad_gain_one = grad_gain_one + gain_part
            grad_bias_one = grad_bias_one + bias_part
            grads[crop_kind] = grads[crop_kind] + value_grad
        layer_grads[layer_index] = (
            grad_gain_one,
            grad_bias_one,
            grad_filter,
            grad_gain_two,
            grad_bias_two,
            grad_weight_one,
            grad_bias_hidden,
            grad_weight_two,
            grad_bias_out,
        )
    stacked = [
        jnp.stack([layer_grads[layer_index][member] for layer_index in range(LAYERS)])
        for member in range(9)
    ]
    summed = lax.psum(
        (
            stacked[0],
            stacked[1],
            stacked[2],
            stacked[3],
            stacked[4],
            stacked[5],
            stacked[6],
            stacked[7],
            stacked[8],
        ),
        ("batch", "rows"),
    )
    large_out = (values[0] * masks[0])[:, None]
    small_out = (values[1] * masks[1])[:, None]
    return (
        large_out,
        small_out,
        grads[0][:, None],
        grads[1][:, None],
        summed[0],
        summed[1],
        summed[2],
        summed[3],
        summed[4],
        summed[5],
        summed[6],
        summed[7],
        summed[8],
    )


def solution(mesh):
    in_specs = (
        P("batch", "rows", None, None, None),
        P("batch", "rows", None, None, None),
        P("batch", "rows", None, None, None),
        P("batch", "rows", None, None, None),
        P("batch", None),
        P(),
        P(),
        P(),
        P(),
        P(),
        P(),
        P(),
        P(),
        P(),
        P(),
        P(),
        P(),
    )
    out_specs = (
        P("batch", "rows", None, None, None),
        P("batch", "rows", None, None, None),
        P("batch", "rows", None, None, None),
        P("batch", "rows", None, None, None),
        P(),
        P(),
        P(),
        P(),
        P(),
        P(),
        P(),
        P(),
        P(),
    )
    return jax.shard_map(local, mesh=mesh, in_specs=in_specs, out_specs=out_specs, check_vma=False)
```

profile of v0, /device:TPU:0, one launch (start us, length us, event | category | flops | bytes accessed | tf_op | source)
XLA Modules:
  0.0 1170.6 jit_solution(15868490597129977744)
XLA Ops:
  20.4 95.5 %all-reduce.16.cloned.1.call-done = bf16[24,2,4,4,8,384]{5,4,3,2,1,0:T(8,128)(2,1)} async-done(((bf16[24,2,4,4,8,384]{5,4,3,2,1,0:T(8,128)(2,1)}), bf16[24,2,4,4,8,384]{5,4,3,2,1,0:T(8,128)(2,1)}) %all-reduce.16.cloned.1.call-update) | async-done | bytes 4718608
  127.3 4.0 copy.323
  138.4 20.5 %all-gather.9.cloned.1.call-done = bf16[24,2,4,4,8,384]{5,4,3,2,0,1:T(8,128)(2,1)} async-done(((bf16[24,2,1,4,8,384]{5,4,3,2,0,1:T(8,128)(2,1)}), bf16[24,2,4,4,8,384]{5,4,3,2,0,1:T(8,128)(2,1)}) %all-gather.9.cloned.1.call-update) | async-done | bytes 4718608 | tf_op jit(solution)/shard_map/all_gather | solution.py:224
  166.9 22.1 %multiply_convert_fusion.1 = (bf16[1344,1536]{1,0:T(8,128)(2,1)S(1)}, f32[1344,1536]{1,0:T(8,128)}, f32[1344,1536]{1,0:T(8,128)}) fusion(f32[1536]{0:T(1024)S(1)} %get-tuple-element.103, bf16[1344,384]{1,0:T(8,128)(2,1)S(1)} %convert_element_type.422, bf16[2,384,1536]{2,1,0:T(8,128)(2,1)} %param.30), kind=kOutput, calls=%fused_computation.27 | convolution fusion | flops 1721696256 | bytes 22861824 | tf_op jit(solution)/shard_map/dot_general | solution.py:236
  189.0 4.4 fusion.199
  198.6 4.8 fusion.25
  213.2 86.4 %all-reduce.18.cloned.1.call-done = bf16[24,2,4,4,8,384]{5,4,3,2,1,0:T(8,128)(2,1)} async-done(((bf16[24,2,4,4,8,384]{5,4,3,2,1,0:T(8,128)(2,1)}), bf16[24,2,4,4,8,384]{5,4,3,2,1,0:T(8,128)(2,1)}) %all-reduce.18.cloned.1.call-update) | async-done | bytes 4718608
  308.3 24.3 %all-gather.13.cloned.1.call-done = bf16[72,2,4,2,4,384]{5,4,3,2,0,1:T(4,128)(2,1)} async-done(((bf16[72,2,1,2,4,384]{5,4,3,2,0,1:T(4,128)(2,1)}), bf16[72,2,4,2,4,384]{5,4,3,2,0,1:T(4,128)(2,1)}) %all-gather.13.cloned.1.call-update) | async-done | bytes 3538960 | tf_op jit(solution)/shard_map/all_gather | solution.py:225
  340.0 15.6 %multiply_convert_fusion.3 = (bf16[864,1536]{1,0:T(8,128)(2,1)S(1)}, f32[864,1536]{1,0:T(8,128)}, f32[864,1536]{1,0:T(8,128)}) fusion(f32[1536]{0:T(1024)S(1)} %get-tuple-element.103, bf16[864,384]{1,0:T(8,128)(2,1)S(1)} %convert_element_type.444, bf16[2,384,1536]{2,1,0:T(8,128)(2,1)} %param.30), kind=kOutput, calls=%fused_computation.67 | convolution fusion | flops 1106804736 | bytes 15120384 | tf_op jit(solution)/shard_map/dot_general | solution.py:236
  363.9 3.9 copy.341
  367.9 4.2 all-gather.11.cloned.1.call-done
  379.5 22.1 %multiply_convert_fusion = (bf16[1344,1536]{1,0:T(8,128)(2,1)S(1)}, f32[1344,1536]{1,0:T(8,128)}, f32[1344,1536]{1,0:T(8,128)}) fusion(f32[1536]{0:T(1024)S(1)} %copy-done.172, bf16[1344,384]{1,0:T(8,128)(2,1)S(1)} %convert_element_type.431, bf16[2,384,1536]{2,1,0:T(8,128)(2,1)} %param.30), kind=kOutput, calls=%fused_computation.14 | convolution fusion | flops 1721696256 | bytes 22861824 | tf_op jit(solution)/shard_map/dot_general | solution.py:236
  410.0 5.4 convert_reduce_fusion.4
  418.8 11.3 convert_reduce_fusion
  430.1 7.0 dot_general.173
  437.1 5.4 fusion.202
  445.2 4.1 fusion.26
  457.6 85.9 %all-reduce.20.cloned.1.call-done = bf16[24,2,4,4,8,384]{5,4,3,2,1,0:T(8,128)(2,1)} async-done(((bf16[24,2,4,4,8,384]{5,4,3,2,1,0:T(8,128)(2,1)}), bf16[24,2,4,4,8,384]{5,4,3,2,1,0:T(8,128)(2,1)}) %all-reduce.20.cloned.1.call-update) | async-done | bytes 4718608
  548.2 28.4 %all-gather.15.cloned.1.call-done = bf16[72,2,4,2,4,384]{5,4,3,2,0,1:T(4,128)(2,1)} async-done(((bf16[72,2,1,2,4,384]{5,4,3,2,0,1:T(4,128)(2,1)}), bf16[72,2,4,2,4,384]{5,4,3,2,0,1:T(4,128)(2,1)}) %all-gather.15.cloned.1.call-update) | async-done | bytes 3538960 | tf_op jit(solution)/shard_map/all_gather | solution.py:225
  584.7 16.0 %multiply_convert_fusion.2 = (bf16[864,1536]{1,0:T(8,128)(2,1)S(1)}, f32[864,1536]{1,0:T(8,128)}, f32[864,1536]{1,0:T(8,128)}) fusion(f32[1536]{0:T(1024)} %get-tuple-element.102, bf16[864,384]{1,0:T(8,128)(2,1)S(1)} %convert_element_type.453, bf16[2,384,1536]{2,1,0:T(8,128)(2,1)} %param.30), kind=kOutput, calls=%fused_computation.54 | convolution fusion | flops 1106804736 | bytes 15122432 | tf_op jit(solution)/shard_map/dot_general | solution.py:236
  607.3 4.5 convert_reduce_fusion.7
  614.9 9.9 convert_reduce_fusion.2
  624.8 5.4 dot_general.183
  630.3 4.7 fusion.203
  647.6 3.9 copy.374
  652.4 4.7 fusion.30
  657.2 35.0 %reduce-scatter.21.cloned.1.call-done = bf16[72,2,1,2,4,384]{5,0,4,3,1,2:T(8,128)(2,1)} async-done(((bf16[72,2,4,2,4,384]{5,0,4,3,1,2:T(8,128)(2,1)}), bf16[72,2,1,2,4,384]{5,0,4,3,1,2:T(8,128)(2,1)}) %reduce-scatter.21.cloned.1.call-update) | async-done | bytes 884752 | tf_op jit(solution)/shard_map/reduce_scatter | solution.py:301
  697.0 3.9 fusion.56
  705.0 11.8 %convert_reduce_fusion.1 = (f32[1536]{0:T(1024)}, bf16[1344,1536]{1,0:T(8,128)(2,1)}) fusion(f32[1344,1536]{1,0:T(8,128)} %get-tuple-element.142, f32[1344,1536]{1,0:T(8,128)} %get-tuple-element.193, bf16[1344,384]{1,0:T(8,128)(2,1)} %convert_element_type.467, bf16[2,1536,384]{2,1,0:T(8,128)(2,1)} %param.32), kind=kOutput, calls=%fused_computation.11 | convolution fusion | flops 1618475520 | bytes 22861824 | tf_op jit(solution)/shard_map/dot_general | solution.py:276
  716.8 7.0 dot_general.178
  723.9 5.6 fusion.204
  732.2 3.9 fusion.27
  736.2 3.8 fusion.42
  753.6 7.9 convert_reduce_fusion.3
  761.5 5.3 dot_general.188
  766.9 5.0 fusion.205
  779.8 3.9 copy.390
  783.8 46.9 %all-reduce.22.cloned.1.call-done = bf16[24,2,4,4,8,384]{5,4,3,2,1,0:T(8,128)(2,1)} async-done(((bf16[24,2,4,4,8,384]{5,4,3,2,1,0:T(8,128)(2,1)}), bf16[24,2,4,4,8,384]{5,4,3,2,1,0:T(8,128)(2,1)}) %all-reduce.22.cloned.1.call-update) | async-done | bytes 4718608
  842.7 4.6 copy.409
  847.2 4.8 fusion.207
  864.1 9.9 reduce-scatter.23.cloned.1.call-done
  879.0 5.8 fusion.50
  886.1 4.0 fusion.208
  902.7 4.5 fusion.49
  929.6 15.9 %all-gather.23.cloned.1.call-done = bf16[72,2,4,2,4,384]{5,4,3,2,0,1:T(4,128)(2,1)} async-done(((bf16[72,2,1,2,4,384]{5,4,3,2,0,1:T(4,128)(2,1)}), bf16[72,2,4,2,4,384]{5,4,3,2,0,1:T(4,128)(2,1)}) %all-gather.23.cloned.1.call-update) | async-done | bytes 3538960 | tf_op jit(solution)/shard_map/all_gather | solution.py:324
  955.4 42.2 %all-reduce.8 = (f32[2,384]{1,0:T(2,128)}, f32[2,384]{1,0:T(2,128)}, f32[2,384]{1,0:T(2,128)}, f32[2,384]{1,0:T(2,128)}, f32[2,1536]{1,0:T(2,128)}, /*index=5*/f32[2,384]{1,0:T(2,128)}) all-reduce(f32[2,384]{1,0:T(2,128)S(1)} %pad_maximum_fusion.16, ...), channel_id=1, replica_groups=mesh['batch'=8,'rows'=4] {'batch','rows'}, use_global_device_ids=true, to_apply=%region_44.45 | all-reduce | flops 6912 | bytes 55296 | tf_op jit(solution)/shard_map/psum | solution.py:350
  997.6 156.8 %all-reduce.24.cloned.1.call-done = (f32[2,2,14,8,384]{4,3,2,1,0:T(8,128)}, f32[2,384,1536]{2,1,0:T(8,128)}, f32[2,1536,384]{2,1,0:T(8,128)}) async-done(((f32[2,2,14,8,384]{4,3,2,1,0:T(8,128)}, f32[2,384,1536]{2,1,0:T(8,128)}, f32[2,1536,384]{2,1,0:T(8,128)}), (f32[2,2,14,8,384]{4,3,2,1,0:T(8,128)}, f32[2,384,1536]{2,1,0:T(8,128)}, f32[2,1536,384]{2,1,0:T(8,128)})) %all-reduce.24.cloned.1.call-update) | async-done | bytes 10125328 | tf_op jit(solution)/shard_map/psum | solution.py:350
  1156.5 4.9 copy.851
  (732 shorter events, 252.7 us)
Async XLA Ops:
  7.2 197.8 %copy-start = (f32[6,14]{1,0:T(8,128)S(1)}, f32[6,14]{1,0:T(8,128)}, u32[]{:S(2)}) copy-start(f32[6,14]{1,0:T(8,128)} %param.23) | copy-start | bytes 1012
  7.2 108.7 %all-reduce.16.cloned.1.call-start = ((), (), s32[]{:S(2)}) async-start(), calls=%async_computation.16 | async-start | bytes 9437184
  14.3 110.5 %copy-start.130 = (f32[384]{0:T(512)}, f32[384]{0:T(512)S(1)}, u32[]{:S(2)}) copy-start(f32[384]{0:T(512)S(1)} %get-tuple-element.216) | copy-start | bytes 4612
  14.3 346.9 %copy-start.139 = (f32[384]{0:T(512)}, f32[384]{0:T(512)S(1)}, u32[]{:S(2)}) copy-start(f32[384]{0:T(512)S(1)} %get-tuple-element.215) | copy-start | bytes 4612
  15.6 183.0 %copy-start.55 = (bf16[2,4,4,8,4,14,1]{5,3,4,2,1,0,6:T(8,128)(2,1)}, bf16[2,4,4,8,4,14,1]{5,3,4,2,1,0,6:T(8,128)(2,1)S(1)}, u32[]{:S(2)}) copy-start(bf16[2,4,4,8,4,14,1]{5,3,4,2,1,0,6:T(8,128)(2,1)S(1)} %fusion.142) | copy-start | bytes 86020
  19.1 139.8 %all-gather.9.cloned.1.call-start = ((), (), s32[]{:S(2)}) async-start(), calls=%async_computation.4 | async-start | bytes 5898240 | tf_op jit(solution)/shard_map/all_gather | solution.py:224
  20.4 99.5 %copy-start.100 = (f32[4,8,384]{2,1,0:T(8,128)}, f32[4,8,384]{2,1,0:T(8,128)S(1)}, u32[]{:S(2)}) copy-start(f32[4,8,384]{2,1,0:T(8,128)S(1)} %get-tuple-element.175) | copy-start | bytes 147460
  20.4 99.5 %copy-start.102 = (f32[4,8,384]{2,1,0:T(8,128)}, f32[4,8,384]{2,1,0:T(8,128)S(1)}, u32[]{:S(2)}) copy-start(f32[4,8,384]{2,1,0:T(8,128)S(1)} %get-tuple-element.176) | copy-start | bytes 147460
  121.2 85.5 %reduce-scatter.17.cloned.1.call-start = ((), (), s32[]{:S(2)}) async-start(), calls=%async_computation.6 | async-start | bytes 4423680 | tf_op jit(solution)/shard_map/reduce_scatter | solution.py:210
  131.4 168.1 %all-reduce.18.cloned.1.call-start = ((), (), s32[]{:S(2)}) async-start(), calls=%async_computation.17 | async-start | bytes 9437184
  133.3 206.7 %copy-start.169 = (f32[1536]{0:T(1024)}, f32[1536]{0:T(1024)S(1)}, u32[]{:S(2)}) copy-start(f32[1536]{0:T(1024)S(1)} %get-tuple-element.103) | copy-start | bytes 18436
  133.4 25.5 %copy-start.58 = (bf16[2,4,4,8,4,14,1]{5,3,4,2,1,0,6:T(8,128)(2,1)}, bf16[2,4,4,8,4,14,1]{5,3,4,2,1,0,6:T(8,128)(2,1)S(1)}, u32[]{:S(2)}) copy-start(bf16[2,4,4,8,4,14,1]{5,3,4,2,1,0,6:T(8,128)(2,1)S(1)} %fusion.143) | copy-start | bytes 86020
  138.4 198.7 %copy-start.124 = (f32[384]{0:T(512)}, f32[384]{0:T(512)S(1)}, u32[]{:S(2)}) copy-start(f32[384]{0:T(512)S(1)} %get-tuple-element.219) | copy-start | bytes 4612
  166.8 22.1 %copy-start.40 = (bf16[1344,384]{1,0:T(8,128)(2,1)}, bf16[1344,384]{1,0:T(8,128)(2,1)S(1)}, u32[]{:S(2)}) copy-start(bf16[1344,384]{1,0:T(8,128)(2,1)S(1)} %convert_element_type.422) | copy-start | bytes 3096580
  166.8 22.1 %copy-start.63 = (f32[1344,384]{1,0:T(8,128)S(1)}, f32[1344,384]{1,0:T(8,128)}, u32[]{:S(2)}) copy-start(f32[1344,384]{1,0:T(8,128)} %reshape.1760) | copy-start | bytes 6193156
  166.8 22.1 %copy-start.190 = (bf16[2,1536,384]{2,1,0:T(8,128)(2,1)S(1)}, bf16[2,1536,384]{2,1,0:T(8,128)(2,1)}, u32[]{:S(2)}) copy-start(bf16[2,1536,384]{2,1,0:T(8,128)(2,1)} %param.32) | copy-start | bytes 7077892
  203.5 129.1 %all-gather.13.cloned.1.call-start = ((), (), s32[]{:S(2)}) async-start(), calls=%async_computation.7 | async-start | bytes 4423680 | tf_op jit(solution)/shard_map/all_gather | solution.py:225
  211.5 160.6 %all-gather.11.cloned.1.call-start = ((), (), s32[]{:S(2)}) async-start(), calls=%async_computation.5 | async-start | bytes 5898240 | tf_op jit(solution)/shard_map/all_gather | solution.py:224
  213.1 90.3 %copy-start.104 = (f32[4,8,384]{2,1,0:T(8,128)}, f32[4,8,384]{2,1,0:T(8,128)S(1)}, u32[]{:S(2)}) copy-start(f32[4,8,384]{2,1,0:T(8,128)S(1)} %get-tuple-element.173) | copy-start | bytes 147460
  213.1 90.3 %copy-start.106 = (f32[4,8,384]{2,1,0:T(8,128)}, f32[4,8,384]{2,1,0:T(8,128)S(1)}, u32[]{:S(2)}) copy-start(f32[4,8,384]{2,1,0:T(8,128)S(1)} %get-tuple-element.174) | copy-start | bytes 147460
  304.6 145.5 %reduce-scatter.19.cloned.1.call-start = ((), (), s32[]{:S(2)}) async-start(), calls=%async_computation.8 | async-start | bytes 4423680 | tf_op jit(solution)/shard_map/reduce_scatter | solution.py:210
  306.7 29.5 %copy-start.155 = (bf16[2,4,2,4,2,6,1]{5,3,4,2,1,0,6:T(4,128)(2,1)}, bf16[2,4,2,4,2,6,1]{5,3,4,2,1,0,6:T(4,128)(2,1)S(1)}, u32[]{:S(2)}) copy-start(bf16[2,4,2,4,2,6,1]{5,3,4,2,1,0,6:T(4,128)(2,1)S(1)} %fusion.168) | copy-start | bytes 4612
  367.8 175.7 %all-reduce.20.cloned.1.call-start = ((), (), s32[]{:S(2)}) async-start(), calls=%async_computation.18 | async-start | bytes 9437184
  379.4 22.2 %copy-start.42 = (bf16[1344,384]{1,0:T(8,128)(2,1)}, bf16[1344,384]{1,0:T(8,128)(2,1)S(1)}, u32[]{:S(2)}) copy-start(bf16[1344,384]{1,0:T(8,128)(2,1)S(1)} %convert_element_type.431) | copy-start | bytes 3096580
  379.4 24.0 %copy-start.184 = (f32[384]{0:T(512)S(1)}, f32[384]{0:T(512)}, u32[]{:S(2)}) copy-start(f32[384]{0:T(512)} %get-tuple-element.104) | copy-start | bytes 4612
  379.5 24.0 %copy-start.192 = (bf16[2,1536,384]{2,1,0:T(8,128)(2,1)S(1)}, bf16[2,1536,384]{2,1,0:T(8,128)(2,1)}, u32[]{:S(2)}) copy-start(bf16[2,1536,384]{2,1,0:T(8,128)(2,1)} %param.32) | copy-start | bytes 7077892
  449.4 127.2 %all-gather.15.cloned.1.call-start = ((), (), s32[]{:S(2)}) async-start(), calls=%async_computation.9 | async-start | bytes 4423680 | tf_op jit(solution)/shard_map/all_gather | solution.py:225
  454.9 196.7 %all-gather.17.cloned.1.call-start = ((), (), s32[]{:S(2)}) async-start(), calls=%async_computation.10 | async-start | bytes 5898240 | tf_op jit(solution)/shard_map/all_gather | solution.py:323
  457.6 88.1 %copy-start.20 = (f32[24,2,1,4,8,384]{5,4,3,2,0,1:T(8,128)S(1)}, f32[24,2,1,4,8,384]{5,4,3,2,0,1:T(8,128)}, u32[]{:S(2)}) copy-start(f32[24,2,1,4,8,384]{5,4,3,2,0,1:T(8,128)} %copy-done.19) | copy-start | bytes 7077892
  457.6 88.1 %copy-start.105 = (f32[4,8,384]{2,1,0:T(8,128)S(1)}, f32[4,8,384]{2,1,0:T(8,128)}, u32[]{:S(2)}) copy-start(f32[4,8,384]{2,1,0:T(8,128)} %copy-done.104) | copy-start | bytes 147460
  457.6 88.1 %copy-start.107 = (f32[4,8,384]{2,1,0:T(8,128)S(1)}, f32[4,8,384]{2,1,0:T(8,128)}, u32[]{:S(2)}) copy-start(f32[4,8,384]{2,1,0:T(8,128)} %copy-done.106) | copy-start | bytes 147460
  547.0 29.6 %copy-start.156 = (bf16[2,4,2,4,2,6,1]{5,3,4,2,1,0,6:T(4,128)(2,1)S(1)}, bf16[2,4,2,4,2,6,1]{5,3,4,2,1,0,6:T(4,128)(2,1)}, u32[]{:S(2)}) copy-start(bf16[2,4,2,4,2,6,1]{5,3,4,2,1,0,6:T(4,128)(2,1)} %copy-done.155) | copy-start | bytes 4612
  548.2 144.0 %reduce-scatter.21.cloned.1.call-start = ((), (), s32[]{:S(2)}) async-start(), calls=%async_computation.12 | async-start | bytes 4423680 | tf_op jit(solution)/shard_map/reduce_scatter | solution.py:301
  584.6 17.5 %copy-start.185 = (f32[384]{0:T(512)S(1)}, f32[384]{0:T(512)}, u32[]{:S(2)}) copy-start(f32[384]{0:T(512)} %get-tuple-element.104) | copy-start | bytes 4612
  651.5 84.7 %all-gather.21.cloned.1.call-start = ((), (), s32[]{:S(2)}) async-start(), calls=%async_computation.13 | async-start | bytes 4423680 | tf_op jit(solution)/shard_map/all_gather | solution.py:324
  657.2 36.5 %copy-start.33 = (f32[72,2,1,2,4,384]{5,4,3,2,0,1:T(4,128)S(1)}, f32[72,2,1,2,4,384]{5,4,3,2,0,1:T(4,128)}, u32[]{:S(2)}) copy-start(f32[72,2,1,2,4,384]{5,4,3,2,0,1:T(4,128)} %copy-done.32) | copy-start | bytes 5308420
  657.2 36.5 %copy-start.123 = (f32[2,4,384]{2,1,0:T(4,128)S(1)}, f32[2,4,384]{2,1,0:T(4,128)}, u32[]{:S(2)}) copy-start(f32[2,4,384]{2,1,0:T(4,128)} %copy-done.122) | copy-start | bytes 36868
  696.9 133.8 %all-reduce.22.cloned.1.call-start = ((), (), s32[]{:S(2)}) async-start(), calls=%async_computation.19 | async-start | bytes 9437184
  736.2 137.8 %reduce-scatter.23.cloned.1.call-start = ((), (), s32[]{:S(2)}) async-start(), calls=%async_computation.14 | async-start | bytes 4423680 | tf_op jit(solution)/shard_map/reduce_scatter | solution.py:301
  783.8 49.1 %copy-start.16 = (f32[24,2,1,4,8,384]{5,4,3,2,0,1:T(8,128)S(1)}, f32[24,2,1,4,8,384]{5,4,3,2,0,1:T(8,128)}, u32[]{:S(2)}) copy-start(f32[24,2,1,4,8,384]{5,4,3,2,0,1:T(8,128)} %copy-done.15) | copy-start | bytes 7077892
  783.8 49.1 %copy-start.101 = (f32[4,8,384]{2,1,0:T(8,128)S(1)}, f32[4,8,384]{2,1,0:T(8,128)}, u32[]{:S(2)}) copy-start(f32[4,8,384]{2,1,0:T(8,128)} %copy-done.100) | copy-start | bytes 147460
  783.8 49.1 %copy-start.103 = (f32[4,8,384]{2,1,0:T(8,128)S(1)}, f32[4,8,384]{2,1,0:T(8,128)}, u32[]{:S(2)}) copy-start(f32[4,8,384]{2,1,0:T(8,128)} %copy-done.102) | copy-start | bytes 147460
  783.8 134.6 %all-gather.19.cloned.1.call-start = ((), (), s32[]{:S(2)}) async-start(), calls=%async_computation.11 | async-start | bytes 5898240 | tf_op jit(solution)/shard_map/all_gather | solution.py:323
  835.4 110.2 %all-gather.23.cloned.1.call-start = ((), (), s32[]{:S(2)}) async-start(), calls=%async_computation.15 | async-start | bytes 4423680 | tf_op jit(solution)/shard_map/all_gather | solution.py:324
  878.7 275.7 %all-reduce.24.cloned.1.call-start = ((), (), s32[]{:S(2)}) async-start(), calls=%async_computation.20 | async-start | bytes 20250624 | tf_op jit(solution)/shard_map/psum | solution.py:350
  926.7 18.8 %copy-start.154 = (bf16[2,4,2,4,2,6,1]{5,3,4,2,1,0,6:T(4,128)(2,1)S(1)}, bf16[2,4,2,4,2,6,1]{5,3,4,2,1,0,6:T(4,128)(2,1)}, u32[]{:S(2)}) copy-start(bf16[2,4,2,4,2,6,1]{5,3,4,2,1,0,6:T(4,128)(2,1)} %copy-done.152) | copy-start | bytes 4612
  929.6 19.7 %copy-start.7 = (bf16[72,1,2,6,384]{4,2,3,1,0:T(2,128)(2,1)S(1)}, bf16[72,1,2,6,384]{4,2,3,1,0:T(2,128)(2,1)}, u32[]{:S(2)}) copy-start(bf16[72,1,2,6,384]{4,2,3,1,0:T(2,128)(2,1)} %param.18) | copy-start | bytes 1990660
  929.6 19.7 %copy-start.66 = (f32[72,2,6]{2,0,1:T(8,128)S(1)}, f32[72,2,6]{2,0,1:T(8,128)}, u32[]{:S(2)}) copy-start(f32[72,2,6]{2,0,1:T(8,128)} %copy-done.65) | copy-start | bytes 10372
  (173 other events, 623.6 us)
Sparse Core Ops, SparseCore 0:
  19.2 96.7 all-reduce.15
  121.3 37.6 all-gather.8
  162.1 40.4 reduce-scatter.16
  205.5 94.0 all-reduce.17
  301.6 30.8 all-gather.12
  334.6 37.4 all-gather.10
  374.8 40.4 reduce-scatter.18
  449.5 93.9 all-reduce.19
  545.7 30.8 all-gather.14
  578.6 37.4 all-gather.16
  651.6 40.4 reduce-scatter.20
  697.0 30.7 all-gather.20
  736.3 94.3 all-reduce.21
  833.3 40.5 reduce-scatter.22
  875.3 37.4 all-gather.18
  914.8 30.7 all-gather.22
  952.9 201.4 all-reduce.23
where the time goes:
time: 1180 us; the launch traced here: 1170 us
  waiting for transfers between devices  610 us (52%)
  matrix products  241 us (20%)
  local copies, waits for them, and re-layouts  145 us (12%)
  other arithmetic  110 us (9%)
  blocking collectives  42.2 us (4%)
  between operations  19.9 us (2%)
    unnamed x21, waiting for transfers between devices  315 us
    psum x1, waiting for transfers between devices, local(): lax.psum((stacked[0], stacked[1], stacked[2], stacked[3], stacked[4], sta...  157 us
    dot_general x4, matrix products, local(): jnp.dot(second_flat, fc1_weight[layer_index], preferred_element_type=jnp....  75.8 us
    all_gather x2, waiting for transfers between devices, local(): lax.all_gather(filtered[1], 'rows', axis=2, tiled=True)  52.6 us
    reduce_scatter x2, waiting for transfers between devices, local(): lax.psum_scatter(band_grads[1].astype(jnp.bfloat16), 'rows', scatter_dime...  44.8 us
    unnamed x416, local copies, waits for them, and re-layouts  44.1 us
    psum x1, blocking collectives, local(): lax.psum((stacked[0], stacked[1], stacked[2], stacked[3], stacked[4], sta...  42.2 us
    dot_general x4, matrix products, local(): jnp.dot(out_grad, fc2_weight[layer_index].T, preferred_element_type=jnp.f...  40.9 us
  transfers between devices with their start and end apart: 17, of which 12 were waited for; matrix products, arithmetic and copies ran while one was open for 38% of the time, Pallas kernels for 0%

commit v1 on v0

v1 whole, which is shorter than its diff:
```python
import math
from functools import partial
import numpy as np
import jax
import jax.numpy as jnp
from jax import lax
from jax.experimental import pallas as pl
from jax.experimental.pallas import tpu as pltpu
from jax.sharding import PartitionSpec as P

D, FF = 384, 1536
HL, WL, FL = 14, 14, 8
HS, WS, FS = 6, 6, 4
BL, BS = 4, 2
LAYERS = 2
EPS = 1e-6
TL, TS = HL * WL, HS * WS
PER = 3
T = TL + PER * TS
CUT, END = 192, 208
NL, NS = HL * FL, HS * FS
BAND = 96
CH = 512
CB = 512
SMALL = 512
MESH = pl.DeviceIdType.MESH
VMEM_LIMIT = 60 * 2**20
F32, BF16 = jnp.float32, jnp.bfloat16
HIGHEST = lax.Precision.HIGHEST


def table(height, width, count):
    k = np.arange(height)[:, None, None, None]
    l = np.arange(count)[None, :, None, None]
    s = np.arange(height)[None, None, :, None]
    w = np.arange(width)[None, None, None, :]
    phase = (k * s * width + l * w * height) % (height * width)
    angle = phase.astype(np.float32) * np.float32(2.0 * math.pi / (height * width))
    scale = np.float32(1.0 / math.sqrt(height * width))
    both = np.stack([np.cos(angle) * scale, -np.sin(angle) * scale])
    return both.reshape(2, height * count, height * width).astype(jnp.bfloat16).astype(np.float32)


def tables():
    large = np.zeros((2 * NL, END), np.float32)
    large[:, :TL] = table(HL, WL, FL).reshape(2 * NL, TL)
    one = table(HS, WS, FS)
    small = np.zeros((2, PER, NS, T - CUT), np.float32)
    for at in range(PER):
        small[:, at, :, TL - CUT + at * TS : TL - CUT + (at + 1) * TS] = one
    small = small.reshape(2 * PER * NS, T - CUT)
    return [jnp.asarray(t, BF16) for t in (large, small, large.T, small.T)]


def normal(x):
    mean = jnp.mean(x, axis=-1, keepdims=True)
    centred = x - mean
    scale = lax.rsqrt(jnp.mean(centred * centred, axis=-1, keepdims=True) + EPS)
    return centred * scale, scale


def normal_back(grad, gain, unit, scale):
    inner = grad * gain
    first = jnp.mean(inner, axis=-1, keepdims=True)
    second = jnp.mean(inner * unit, axis=-1, keepdims=True)
    return (inner - first - unit * second) * scale


def dot(a, b):
    return jnp.dot(a, b, preferred_element_type=F32)


def dot_nt(a, b):
    return lax.dot_general(a, b, (((1,), (1,)), ((), ())), preferred_element_type=F32)


def dot_tn(a, b):
    return lax.dot_general(a, b, (((0,), (0,)), ((), ())), preferred_element_type=F32)


def analyse(large_table, small_table, values):
    return dot(large_table, values[:END]), dot(small_table, values[CUT:])


def synthesise(large_back, small_back, large, small):
    a, b = dot(large_back, large), dot(small_back, small)
    return jnp.concatenate([a[:CUT], a[CUT:] + b[: END - CUT], b[END - CUT :]], axis=0)


def thrice(x):
    return jnp.concatenate([x] * PER, axis=0)


def gelu_both(h):
    cdf = 0.5 + 0.5 * lax.erf(h * np.float32(math.sqrt(0.5)))
    dens = jnp.exp(h * h * np.float32(-0.5)) * np.float32(1 / math.sqrt(2 * math.pi))
    return h * cdf, cdf + h * dens


def live_rows(live, group):
    t = lax.broadcasted_iota(jnp.int32, (T, 1), 0)
    mask = jnp.where(t < TL, live[group, 0], live[group, PER])
    for at in range(PER - 1):
        mask = jnp.where((t >= TL + at * TS) & (t < TL + (at + 1) * TS), live[group, 1 + at], mask)
    return mask


def whole(shape):
    return pl.BlockSpec(shape, lambda *a: (0,) * len(shape))


def scalars():
    return pl.BlockSpec(memory_space=pltpu.SMEM)


def forward_kernel(row_count, groups, pair, packed_in, packed_cot, live, pick, place, gain1, bias1, filt_l, filt_s, gain2, bias2,
                   w1, b1, w2, b2, tl, ts, tlb, tsb, outs, xs, zs, spec, vs, gs, ps, do,
                   slots, own_sem, send_sem, recv_sem):
    step = pl.program_id(0)
    batch, row = lax.axis_index("batch"), lax.axis_index("rows")
    last = groups // pair - 1

    def remote(which, m, g):
        to = (row + m) % row_count
        given = (packed_in, packed_cot)[which]
        return pltpu.make_async_remote_copy(
            src_ref=given.at[to * groups + g], dst_ref=slots.at[which, m, g],
            send_sem=send_sem.at[which, m - 1, g], recv_sem=recv_sem.at[which, m - 1, g],
            device_id=(batch, to), device_id_type=MESH)

    def mine(which, g):
        given = (packed_in, packed_cot)[which]
        return pltpu.make_async_copy(given.at[row * groups + g], slots.at[which, 0, g], own_sem.at[which, g])

    @pl.when(step == 0)
    def _():
        barrier = pltpu.get_barrier_semaphore()
        for m in range(1, row_count):
            pl.semaphore_signal(barrier, inc=1, device_id=(batch, (row + m) % row_count), device_id_type=MESH)
        for which in range(2):
            @pl.loop(0, groups)
            def _(g):
                mine(which, g).start()
        pl.semaphore_wait(barrier, row_count - 1)
        for which in range(2):
            @pl.loop(0, groups)
            def _(g):
                for m in range(1, row_count):
                    remote(which, m, g).start()

    def take(which, g):
        mine(which, g).wait()
        for m in range(1, row_count):
            remote(which, m, g).wait_recv()
        return dot(pick[...], jnp.concatenate([slots[which, m, g] for m in range(row_count)], axis=0))

    x = [take(0, step * pair + j) for j in range(pair)]
    for n in range(LAYERS):
        v = []
        for j in range(pair):
            xs[n, j] = x[j]
            u, _ = normal(x[j])
            u = (u * gain1[n : n + 1] + bias1[n : n + 1]).astype(BF16)
            xl, xsm = analyse(tl[...], ts[...], u)
            spec[n, j, : 2 * NL] = xl
            spec[n, j, 2 * NL :] = xsm
            lr, li = xl[:NL], xl[NL:]
            sr, si = xsm[: PER * NS], xsm[PER * NS :]
            gr, gi = filt_l[n, 0], filt_l[n, 1]
            yl = jnp.concatenate([lr * gr - li * gi, lr * gi + li * gr], axis=0).astype(BF16)
            gr, gi = thrice(filt_s[n, 0]), thrice(filt_s[n, 1])
            ys = jnp.concatenate([sr * gr - si * gi, sr * gi + si * gr], axis=0).astype(BF16)
            z = synthesise(tlb[...], tsb[...], yl, ys)
            zs[n, j] = z
            q, _ = normal(z)
            q = (q * gain2[n : n + 1] + bias2[n : n + 1]).astype(BF16)
            vs[n, j] = q
            v.append(q)
        v = jnp.concatenate(v, axis=0)
        total = jnp.concatenate(x, axis=0) + b2[n : n + 1]
        for c in range(0, FF, CH):
            h = dot(v, w1[n, :, c : c + CH]) + b1[n : n + 1, c : c + CH]
            g, slope = gelu_both(h)
            g = g.astype(BF16)
            slope = slope.astype(BF16)
            for j in range(pair):
                gs[n, j, :, c : c + CH] = g[j * T : (j + 1) * T]
                ps[n, j, :, c : c + CH] = slope[j * T : (j + 1) * T]
            total = total + dot(g, w2[n, c : c + CH, :])
        x = [total[j * T : (j + 1) * T] for j in range(pair)]
    for j in range(pair):
        spread = dot(place[...], (x[j] * live_rows(live, step * pair + j)).astype(BF16)).astype(BF16)
        for m in range(row_count):
            outs[m, j] = spread[m * BAND : (m + 1) * BAND]

    @pl.when(step == last)
    def _():
        for g in range(groups):
            do[g] = (take(1, g) * live_rows(live, g)).astype(BF16)
        for which in range(2):
            @pl.loop(0, groups)
            def _(g):
                for m in range(1, row_count):
                    remote(which, m, g).wait_send()


def forward(mesh, groups, pair, packed_in, packed_cot, live, small):
    rows = mesh.shape["rows"]
    sizes = [(T, D, F32), (T, D, F32), (2 * NL + 2 * PER * NS, D, F32), (T, D, BF16), (T, FF, BF16), (T, FF, BF16)]
    hbm = pl.BlockSpec(memory_space=pl.ANY)
    return pl.pallas_call(
        partial(forward_kernel, rows, groups, pair),
        grid=(groups // pair,),
        in_specs=[hbm, hbm, scalars()] + [whole(a.shape) for a in small],
        out_specs=[pl.BlockSpec((rows, pair, BAND, D), lambda i: (0, i, 0, 0))]
        + [pl.BlockSpec((LAYERS, pair, a, b), lambda i: (0, i, 0, 0)) for a, b, _ in sizes]
        + [whole((groups, T, D))],
        out_shape=[jax.ShapeDtypeStruct((rows, groups, BAND, D), BF16)]
        + [jax.ShapeDtypeStruct((LAYERS, groups, a, b), t) for a, b, t in sizes]
        + [jax.ShapeDtypeStruct((groups, T, D), BF16)],
        scratch_shapes=[pltpu.VMEM((2, rows, groups, BAND, D), BF16), pltpu.SemaphoreType.DMA((2, groups)),
                        pltpu.SemaphoreType.DMA((2, rows - 1, groups)), pltpu.SemaphoreType.DMA((2, rows - 1, groups))],
        compiler_params=pltpu.CompilerParams(collective_id=1, has_side_effects=True, vmem_limit_bytes=VMEM_LIMIT),
        name="forward",
    )(packed_in, packed_cot, live, *small)


LOW = 2


def add_rows(target, at_target, base, sources, count):
    step = next(s for s in (128, 96, 64, 48, 32, 16) if count % s == 0)

    @pl.loop(0, count // step)
    def _(i):
        at = pl.multiple_of(i * step, 16)
        rows = pl.ds(pl.multiple_of(base + at, 16), step)
        total = at_target[rows, :].astype(F32)
        for ref in sources:
            total = total + ref[pl.ds(at, step), :].astype(F32)
        target[rows, :] = total.astype(BF16)


class Sum:
    def __init__(self, mesh_rows, mesh_batch, acc, full, out, count, bufs, sems, save_sem):
        self.batch, self.row = lax.axis_index("batch"), lax.axis_index("rows")
        self.x_n, self.z_n = mesh_rows // 2, mesh_batch // LOW
        self.acc, self.full, self.out, self.count, self.bufs, self.sems, self.save_sem = acc, full, out, count, bufs, sems, save_sem
        core, x, z, y = self.row % 2, self.row // 2, self.batch // LOW, self.batch % LOW
        self.size = kinds(mesh_rows, mesh_batch)
        self.me = [core, y, z * self.x_n + x]

    def other(self, level, step):
        core, x, z, y = self.row % 2, self.row // 2, self.batch // LOW, self.batch % LOW
        at = (self.me[level] + step) % self.size[level]
        if level == 0:
            return (self.batch, x * 2 + at), at
        if level == 1:
            return (z * LOW + at, self.row), at
        return ((at // self.x_n) * LOW + y, (at % self.x_n) * 2 + core), at

    def region(self, part, level):
        base, count = part * self.count, self.count
        for i in range(level):
            count //= self.size[i]
            base = base + self.me[i] * count
        return base, count

    def rows(self, base, count):
        return pl.ds(pl.multiple_of(base, 16), count)

    def down(self, part, level, step):
        base, count = self.region(part, level)
        device, at = self.other(level, step)
        chunk = count // self.size[level]
        return pltpu.make_async_remote_copy(
            src_ref=self.acc.at[self.rows(base + at * chunk, chunk)], dst_ref=self.bufs[level].at[part, step - 1],
            send_sem=self.sems[level].at[0, part, step - 1], recv_sem=self.sems[level].at[1, part, step - 1],
            device_id=device, device_id_type=MESH)

    def up(self, part, level, step, arriving=False):
        base, count = self.region(part, level + 1)
        device, _ = self.other(level, step)
        if arriving:
            low, _ = self.region(part, level)
            base = low + (self.me[level] - step + self.size[level]) % self.size[level] * count
        rows = self.rows(base, count)
        return pltpu.make_async_remote_copy(
            src_ref=self.full.at[rows], dst_ref=self.full.at[rows],
            send_sem=self.sems[level].at[2, part, step - 1], recv_sem=self.sems[level].at[3, part, step - 1],
            device_id=device, device_id_type=MESH)

    def save(self, part):
        rows = self.rows(part * self.count, self.count)
        return pltpu.make_async_copy(self.full.at[rows], self.out.at[rows], self.save_sem.at[part])

    def stage(self, part, k):
        if 1 <= k <= 3:
            level = k - 1
            for step in range(1, self.size[level]):
                self.down(part, level, step).wait()
            base, count = self.region(part, level + 1)
            add_rows(self.full if k == 3 else self.acc, self.acc, base,
                     [self.bufs[level].at[part, s] for s in range(self.size[level] - 1)], count)
        if k < 3:
            for step in range(1, self.size[k]):
                self.down(part, k, step).start()
        if k >= 4:
            level = 6 - k
            for step in range(1, self.size[level]):
                self.up(part, level, step).wait_send()
                self.up(part, level, step, True).wait_recv()
        if 3 <= k < 6:
            for step in range(1, self.size[5 - k]):
                self.up(part, 5 - k, step).start()
        if k == 6:
            self.save(part).start()


def kinds(mesh_rows, mesh_batch):
    size = [2, LOW, (mesh_rows // 2) * (mesh_batch // LOW)]
    return size


def columns(mesh_rows, mesh_batch):
    sizes = {w: w * padded(mesh_rows, mesh_batch, 2 * D * (CB // w)) for w in (256, 128)}
    return min(sizes, key=sizes.get)


def padded(mesh_rows, mesh_batch, count):
    unit = 16 * math.prod(kinds(mesh_rows, mesh_batch))
    return -(-count // unit) * unit


def sum_scratch(mesh_rows, mesh_batch, parts, count, width):
    size = kinds(mesh_rows, mesh_batch)
    shapes = [pltpu.VMEM((parts * count, width), BF16)] * 2
    for n in size:
        count //= n
        shapes.append(pltpu.VMEM((parts, n - 1, count, width), BF16))
    return shapes + [pltpu.SemaphoreType.DMA((4, parts, n - 1)) for n in size] + [pltpu.SemaphoreType.DMA((parts,))]


def backward_kernel(row_count, batch_count, groups, pair, live, pick, place, gain1, filt_l, filt_s, gain2, w1, w2, tl, ts, tlb, tsb,
                    mix, fold, outs, do_in, xs, zs, spec, vs, gs, ps,
                    out_land, grad_land, weights_out, small_out,
                    dx, dv, do, dot_, vt, dh, gslots, dvec, dhid, dfl, dfs, out_sem, grad_sem, own_sem, *sums):
    i = pl.program_id(0)
    batch, row = lax.axis_index("batch"), lax.axis_index("rows")
    chunks, pairs = FF // CB, groups // pair
    per = chunks + pairs
    compute_steps = LAYERS * per
    layer, q = LAYERS - 1 - i // per, i % per
    width = columns(row_count, batch_count)
    part_rows = padded(row_count, batch_count, 2 * D * (CB // width))
    small_rows = padded(row_count, batch_count, SMALL)
    weights = Sum(row_count, batch_count, sums[0], sums[1], weights_out, part_rows, sums[2:5], sums[5:8], sums[8])
    small = Sum(row_count, batch_count, sums[9], sums[10], small_out, small_rows, sums[11:14], sums[14:17], sums[17])

    def send_out(m, g):
        return pltpu.make_async_remote_copy(
            src_ref=outs.at[m, g], dst_ref=out_land.at[m, g], send_sem=out_sem.at[0, m - 1, g], recv_sem=out_sem.at[1, m - 1, g],
            device_id=(batch, (row - m + row_count) % row_count), device_id_type=MESH)

    def send_grad(m, g):
        return pltpu.make_async_remote_copy(
            src_ref=gslots.at[m, g], dst_ref=grad_land.at[m, g], send_sem=grad_sem.at[0, m - 1, g], recv_sem=grad_sem.at[1, m - 1, g],
            device_id=(batch, (row - m + row_count) % row_count), device_id_type=MESH)

    def keep_out():
        return pltpu.make_async_copy(outs.at[0], out_land.at[0], own_sem.at[0])

    def keep_grad():
        return pltpu.make_async_copy(gslots.at[0], grad_land.at[0], own_sem.at[1])

    @pl.when(i == 0)
    def _():
        barrier = pltpu.get_barrier_semaphore()
        greeted = 0
        for m in range(1, row_count):
            pl.semaphore_signal(barrier, inc=1, device_id=(batch, (row + m) % row_count), device_id_type=MESH)
            greeted += 1
        for level in (1, 2):
            for step in range(1, weights.size[level]):
                pl.semaphore_signal(barrier, inc=1, device_id=weights.other(level, step)[0], device_id_type=MESH)
                greeted += 1
        keep_out().start()
        if part_rows > 2 * D * (CB // width):
            weights.acc[...] = jnp.zeros_like(weights.acc)
        for g in range(groups):
            dx[g] = do_in[g].astype(F32)
        for ref in (dvec, dfl, dfs):
            ref[...] = jnp.zeros_like(ref)
        pl.semaphore_wait(barrier, greeted)

    @pl.when(i < groups)
    def _():
        for m in range(1, row_count):
            send_out(m, i).start()

    @pl.when((i < compute_steps) & (q == 0))
    def _():
        for g in range(groups):
            rows = pl.ds(g * T, T)
            low = dx[g].astype(BF16)
            do[g] = low
            dvec[layer, 4:5] += jnp.sum(low.astype(F32), axis=0, keepdims=True)
        dot_[...] = do[...].reshape(groups * T, D).T
        vt[:D] = vs[0].reshape(groups * T, D).T
        vt[D:] = jnp.ones((16, groups * T), BF16)
        dv[...] = jnp.zeros_like(dv)

    @pl.when((i < compute_steps) & (q < chunks))
    def _():
        for g in range(0, groups, pair):
            rows = slice(g * T, (g + pair) * T)
            some = do[g : g + pair].reshape(pair * T, D)
            slope = ps[0, g : g + pair].reshape(pair * T, CB)
            part = (dot_nt(some, w2[0]) * slope.astype(F32)).astype(BF16)
            dh[rows] = part
            dv[g : g + pair] += dot_nt(part, w1[0]).reshape(pair, T, D)
        part = (LAYERS - 1 - layer) * chunks + q
        base = part * part_rows
        one = dot(vt[...], dh[...])
        dhid[layer, :, pl.ds(pl.multiple_of(q * CB, CB), CB)] = one[D : D + 1]
        two = dot(dot_[...], gs[0].reshape(groups * T, CB))
        for c in range(CB // width):
            cols = slice(c * width, (c + 1) * width)
            weights.acc[weights.rows(base + c * D, D), :] = one[:D, cols].astype(BF16)
            weights.acc[weights.rows(base + (CB // width + c) * D, D), :] = two[:, cols].astype(BF16)

    @pl.when((i < compute_steps) & (q >= chunks))
    def _():
        for j in range(pair):
            g = (q - chunks) * pair + j
            dvg = dv[g]
            u, scale = normal(zs[0, j])
            row_sum = lambda a: jnp.sum(a, axis=0, keepdims=True)
            dvec[layer, 2:3] += row_sum(dvg * u)
            dvec[layer, 3:4] += row_sum(dvg)
            dz = normal_back(dvg, gain2[0], u, scale).astype(BF16)
            yl, ysm = analyse(tl[...], ts[...], dz)
            lr, li = yl[:NL], yl[NL:]
            sr, si = ysm[: PER * NS], ysm[PER * NS :]
            xr, xi = spec[0, j, :NL], spec[0, j, NL : 2 * NL]
            dfl[layer, :NL] += lr * xr + li * xi
            dfl[layer, NL:] += li * xr - lr * xi
            gr, gi = filt_l[0, 0], filt_l[0, 1]
            dl = jnp.concatenate([lr * gr + li * gi, li * gr - lr * gi], axis=0).astype(BF16)
            xr, xi = spec[0, j, 2 * NL : 2 * NL + PER * NS], spec[0, j, 2 * NL + PER * NS :]
            once = lambda a: a[:NS] + a[NS : 2 * NS] + a[2 * NS :]
            dfs[layer, :NS] += once(sr * xr + si * xi)
            dfs[layer, NS:] += once(si * xr - sr * xi)
            gr, gi = thrice(filt_s[0, 0]), thrice(filt_s[0, 1])
            ds = jnp.concatenate([sr * gr + si * gi, si * gr - sr * gi], axis=0).astype(BF16)
            du = synthesise(tlb[...], tsb[...], dl, ds)
            u, scale = normal(xs[0, j])
            dvec[layer, 0:1] += row_sum(du * u)
            dvec[layer, 1:2] += row_sum(du)
            grad = dx[g] + normal_back(du, gain1[0], u, scale)
            dx[g] = grad

            @pl.when(layer == 0)
            def _():
                spread = dot(place[...], grad.astype(BF16)).astype(BF16)
                for m in range(row_count):
                    gslots[m, g] = spread[m * BAND : (m + 1) * BAND]
                for m in range(1, row_count):
                    send_grad(m, g).start()

    @pl.when(i == compute_steps - 1)
    def _():
        small.acc[...] = jnp.zeros_like(small.acc)
        exact = partial(jnp.dot, preferred_element_type=F32, precision=HIGHEST)
        for n in range(LAYERS):
            for c in range(2):
                at = (n * 2 + c) * NL
                small.acc[at : at + NL, :] = (dfl[n, c * NL : (c + 1) * NL] * fold[...]
                                              + exact(mix[...], dfs[n, c * NS : (c + 1) * NS])).astype(BF16)
        at = LAYERS * 2 * NL
        rest = [dvec[n, k : k + 1] for n in range(LAYERS) for k in range(5)]
        rest += [dhid[n, :, c : c + D] for n in range(LAYERS) for c in range(0, FF, D)]
        rest.append(jnp.zeros((-len(rest) % 16, D), F32))
        rest = jnp.concatenate(rest, axis=0).astype(BF16)
        small.acc[at : at + rest.shape[0], :] = rest
        keep_grad().start()

    for k in range(6, -1, -1):
        made = i - k

        @pl.when((made >= 0) & (made < compute_steps) & (made % per < chunks))
        def _():
            weights.stage(made // per * chunks + made % per, k)

        @pl.when(made == compute_steps - 1)
        def _():
            small.stage(0, k)

    @pl.when(i == pl.num_programs(0) - 1)
    def _():
        keep_out().wait()
        keep_grad().wait()
        for m in range(1, row_count):
            @pl.loop(0, groups)
            def _(g):
                send_out(m, g).wait()
                send_grad(m, g).wait()
        for part in range(LAYERS * chunks):
            weights.save(part).wait()
        small.save(0).wait()


def backward(mesh, groups, pair, live, small, tabs, mix, fold, outs, do, saved):
    rows, batch = mesh.shape["rows"], mesh.shape["batch"]
    pick, place, gain1, filt_l, filt_s, gain2, w1, w2 = small
    chunks, pairs = FF // CB, groups // pair
    per, last = chunks + pairs, LAYERS - 1
    steps = LAYERS * per + 6
    layer = lambda i: jnp.maximum(last - i // per, 0)
    when = lambda i: jnp.where(i < LAYERS * per, i % per, per - 1)
    chunk = lambda i: jnp.minimum(when(i), chunks - 1)
    place_of = lambda i: jnp.maximum(when(i) - chunks, 0)
    per_layer = lambda a: pl.BlockSpec((1,) + a.shape[1:], lambda i: (layer(i),) + (0,) * (a.ndim - 1))
    by_pair = lambda a: pl.BlockSpec((1, pair) + a.shape[2:], lambda i: (layer(i), place_of(i), 0, 0))
    by_chunk = lambda a: pl.BlockSpec((1, groups, T, CB), lambda i: (layer(i), 0, 0, chunk(i)))
    gain1, gain2 = gain1[:, None], gain2[:, None]
    xs, zs, spec, vs, gs, ps = saved
    hbm = pl.BlockSpec(memory_space=pl.ANY)
    width = columns(rows, batch)
    part_rows, small_rows = padded(rows, batch, 2 * D * (CB // width)), padded(rows, batch, SMALL)
    dma = pltpu.SemaphoreType.DMA
    return pl.pallas_call(
        partial(backward_kernel, rows, batch, groups, pair),
        grid=(steps,),
        in_specs=[scalars(), whole(pick.shape), whole(place.shape)] + [per_layer(a) for a in (gain1, filt_l, filt_s, gain2)]
        + [pl.BlockSpec((1, D, CB), lambda i: (layer(i), 0, chunk(i))), pl.BlockSpec((1, CB, D), lambda i: (layer(i), chunk(i), 0))]
        + [whole(a.shape) for a in (*tabs, mix, fold)] + [hbm, whole(do.shape)]
        + [by_pair(xs), by_pair(zs), by_pair(spec), per_layer(vs), by_chunk(gs), by_chunk(ps)],
        out_specs=[hbm] * 4,
        out_shape=[jax.ShapeDtypeStruct((rows, groups, BAND, D), BF16)] * 2
        + [jax.ShapeDtypeStruct((LAYERS * chunks * part_rows, width), BF16), jax.ShapeDtypeStruct((small_rows, D), BF16)],
        scratch_shapes=[pltpu.VMEM((groups, T, D), F32), pltpu.VMEM((groups, T, D), F32), pltpu.VMEM((groups, T, D), BF16),
                        pltpu.VMEM((D, groups * T), BF16), pltpu.VMEM((D + 16, groups * T), BF16),
                        pltpu.VMEM((groups * T, CB), BF16), pltpu.VMEM((rows, groups, BAND, D), BF16),
                        pltpu.VMEM((LAYERS, 5, D), F32), pltpu.VMEM((LAYERS, 1, FF), F32),
                        pltpu.VMEM((LAYERS, 2 * NL, D), F32), pltpu.VMEM((LAYERS, 2 * NS, D), F32),
                        dma((2, rows - 1, groups)), dma((2, rows - 1, groups)), dma((2,))]
        + sum_scratch(rows, batch, LAYERS * chunks, part_rows, width) + sum_scratch(rows, batch, 1, small_rows, D),
        compiler_params=pltpu.CompilerParams(collective_id=2, has_side_effects=True, vmem_limit_bytes=VMEM_LIMIT),
        name="backward",
    )(live, pick, place, gain1, filt_l, filt_s, gain2, w1, w2, *tabs, mix, fold, outs, do, xs, zs, spec, vs, gs, ps)


def unpack_kernel(order, outs, grads, weights, small, large_out, small_crops, large_grad, small_grad, dw1, dw2,
                  dfilter, dvec, dhid):
    i = pl.program_id(0)
    for given, large, little in ((outs, large_out, small_crops), (grads, large_grad, small_grad)):
        for g in range(given.shape[1]):
            block = given[0, g].astype(F32)
            for s in range(BL):
                large[g, 0, s] = block[s * WL : (s + 1) * WL]
            for p in range(PER):
                for s in range(BS):
                    at = BL * WL + (p * BS + s) * WS
                    little[g * PER + p, 0, s] = block[at : at + WS]
    width = weights.shape[1]
    parts = CB // width
    for c in range(parts):
        cols = slice(c * width, (c + 1) * width)
        dw1[0, :, cols] = weights[c * D : (c + 1) * D, :].astype(F32)
        dw2[0, cols, :] = weights[(parts + c) * D : (parts + c + 1) * D, :].astype(F32).T

    @pl.when(i == 0)
    def _():
        at = LAYERS * 2 * NL
        for n in range(LAYERS):
            for c in range(2):
                dfilter[n, c] = small[(n * 2 + c) * NL : (n * 2 + c + 1) * NL].astype(F32)
        rest = small[at : at + 32].astype(F32)
        for n in range(LAYERS):
            for k in range(5):
                dvec[k, n : n + 1] = rest[n * 5 + k : n * 5 + k + 1]
            for c in range(FF // D):
                r = LAYERS * 5 + n * (FF // D) + c
                dhid[n : n + 1, c * D : (c + 1) * D] = rest[r : r + 1]


def unpack(mesh, groups, outs, grads, weights, small):
    rows = mesh.shape["rows"]
    me = lax.axis_index("rows")
    crops = rows * groups
    chunks = FF // CB
    parts = LAYERS * chunks
    steps = max(rows, parts)
    order = (jnp.arange(rows, dtype=jnp.int32) - me) % rows
    dev = lambda i: jnp.minimum(i, rows - 1)
    part = lambda i: jnp.minimum(i, parts - 1)
    part_rows = weights.shape[0] // parts
    given = pl.BlockSpec((1, groups, BAND, D), lambda i, order: (order[dev(i)], 0, 0, 0))
    large = pl.BlockSpec((groups, 1, BL, WL, D), lambda i, order: (dev(i), 0, 0, 0, 0))
    little = pl.BlockSpec((groups * PER, 1, BS, WS, D), lambda i, order: (dev(i), 0, 0, 0, 0))
    every = lambda shape: pl.BlockSpec(shape, lambda i, order: (0,) * len(shape))
    large_shape = jax.ShapeDtypeStruct((crops, 1, BL, WL, D), F32)
    little_shape = jax.ShapeDtypeStruct((crops * PER, 1, BS, WS, D), F32)
    shapes = [(LAYERS, 2, NL, D), (5, LAYERS, D), (LAYERS, FF)]
    return pl.pallas_call(
        unpack_kernel,
        grid_spec=pltpu.PrefetchScalarGridSpec(
            num_scalar_prefetch=1, grid=(steps,),
            in_specs=[given, given, pl.BlockSpec((part_rows, weights.shape[1]), lambda i, order: (part(i), 0)), every(small.shape)],
            out_specs=[large, little, large, little,
                       pl.BlockSpec((1, D, CB), lambda i, order: (LAYERS - 1 - part(i) // chunks, 0, part(i) % chunks)),
                       pl.BlockSpec((1, CB, D), lambda i, order: (LAYERS - 1 - part(i) // chunks, part(i) % chunks, 0))]
            + [every(s) for s in shapes]),
        out_shape=[large_shape, little_shape, large_shape, little_shape,
                   jax.ShapeDtypeStruct((LAYERS, D, FF), F32), jax.ShapeDtypeStruct((LAYERS, FF, D), F32)]
        + [jax.ShapeDtypeStruct(s, F32) for s in shapes],
        compiler_params=pltpu.CompilerParams(vmem_limit_bytes=VMEM_LIMIT),
        name="unpack",
    )(order, outs, grads, weights, small)


def token_columns(rows, band_bounds, me):
    t = np.arange(T)
    small = t >= TL
    at = np.where(small, (t - TL) % TS, t)
    wide = np.where(small, WS, WL)
    r, w = jnp.asarray(at // wide, jnp.int32), at % wide
    crop = np.where(small, (t - TL) // TS, 0)
    start = jnp.asarray(np.where(small, BL * WL + crop * BS * WS + w, w), jnp.int32)
    band = (me - jnp.arange(rows, dtype=jnp.int32)) % rows
    first, end = jnp.where(small[:, None], band_bounds[1][band], band_bounds[0][band]), jnp.where(
        small[:, None], band_bounds[1][band + 1], band_bounds[0][band + 1])
    inside = (r[:, None] >= first) & (r[:, None] < end)
    column = start[:, None] + (r[:, None] - first) * jnp.asarray(wide, jnp.int32)[:, None]
    return jnp.where(inside, column, -1)


def local(mesh, large_in, small_in, large_cot, small_cot, crop_counts, band_bounds, row_interp, col_interp,
          norm1_gain, norm1_bias, filters, norm2_gain, norm2_bias, fc1_weight, fc1_bias, fc2_weight, fc2_bias):
    rows = mesh.shape["rows"]
    me = lax.axis_index("rows")
    crops = large_in.shape[0]
    groups = crops // rows
    pair = 2 if groups % 2 == 0 else 1
    tabs = tables()
    column = token_columns(rows, band_bounds, me)
    pick = (column[:, :, None] == jnp.arange(BAND, dtype=jnp.int32)).astype(BF16).reshape(T, rows * BAND)
    place = (column.T[:, None, :] == jnp.arange(BAND, dtype=jnp.int32)[None, :, None]).astype(BF16).reshape(rows * BAND, T)
    at = me * groups + jnp.arange(groups, dtype=jnp.int32)
    live = jnp.concatenate([(at < crop_counts[0, 0])[:, None],
                            (at[:, None] * PER + jnp.arange(PER, dtype=jnp.int32)) < crop_counts[0, 1]], axis=1)
    live = live.astype(F32)

    def pack(large, small):
        return jnp.concatenate([large.reshape(crops, BL * WL, D), small.reshape(crops, PER * BS * WS, D),
                                jnp.zeros((crops, BAND - BL * WL - PER * BS * WS, D), large.dtype)], axis=1)

    small_filter = jnp.einsum("ka,ncabd,lb->nckld", row_interp, filters, col_interp, precision=HIGHEST)
    fold_l = np.where((np.arange(FL) == 0) | (2 * np.arange(FL) == WL), 1.0, 2.0).astype(np.float32)
    fold_s = np.where((np.arange(FS) == 0) | (2 * np.arange(FS) == WS), 1.0, 2.0).astype(np.float32)
    filt_l = (filters * fold_l[:, None]).reshape(LAYERS, 2, NL, D)
    filt_s = (small_filter * fold_s[:, None]).reshape(LAYERS, 2, NS, D)
    mix = jnp.einsum("ka,lb->abkl", row_interp, col_interp * fold_s[:, None]).reshape(NL, NS)
    fold = jnp.asarray(np.tile(fold_l, HL)[:, None])

    outs, *saved, do = forward(mesh, groups, pair, pack(large_in, small_in), pack(large_cot, small_cot), live,
                               (pick, place, norm1_gain, norm1_bias, filt_l, filt_s, norm2_gain, norm2_bias,
                                fc1_weight, fc1_bias, fc2_weight, fc2_bias, *tabs))
    outs, grads, weights, small = backward(
        mesh, groups, pair, live, (pick, place, norm1_gain, filt_l, filt_s, norm2_gain, fc1_weight, fc2_weight), tabs,
        mix, fold, outs, do, saved)
    large_out, small_out, large_grad, small_grad, dw1, dw2, dfilter, dvec, dhid = unpack(
        mesh, groups, outs, grads, weights, small)
    return (large_out, small_out, large_grad, small_grad, dvec[0], dvec[1], dfilter.reshape(filters.shape), dvec[2], dvec[3],
            dw1, dhid, dw2, dvec[4])


def solution(mesh):
    split = P("batch", "rows", None, None, None)
    return jax.shard_map(partial(local, mesh), mesh=mesh, in_specs=(split,) * 4 + (P("batch", None),) + (P(),) * 12,
                         out_specs=(split,) * 4 + (P(),) * 9, check_vma=False)
```

time: 1180 us -> 222 us (0.19)
  waiting for transfers between devices: 610 us -> 0 us
  matrix products: 241 us -> 1.05 us
  Pallas kernels: 0 us -> 186 us
  local copies, waits for them, and re-layouts: 145 us -> 23.3 us
  other arithmetic: 110 us -> 10.7 us
  blocking collectives: 42.2 us -> 0 us
  between operations: 19.9 us -> 0.89 us
    unnamed x21 -> x0, waiting for transfers between devices: 315 us -> none
    dot_general x48 -> x2, matrix products: 241 us -> 1.05 us  [local(): jnp.einsum('ka,ncabd,lb->nckld', row_interp, filters, col_interp, precisi...]
    pallas_call x0 -> x3, Pallas kernels: none -> 186 us  [the longest x1 122 us: backward(): pl.pallas_call(partial(backward_kernel, rows, batch, groups, pair), grid=...]
    psum x1 -> x0, waiting for transfers between devices: 157 us -> none  [local(): lax.psum((stacked[0], stacked[1], stacked[2], stacked[3], stacked[4], sta...]
    all_gather x8 -> x0, waiting for transfers between devices: 93.3 us -> none  [the longest x2 52.6 us: local(): lax.all_gather(filtered[1], 'rows', axis=2, tiled=True)]
    reduce_sum x42 -> x0, other arithmetic: 56.6 us -> none  [the longest x18 24.9 us: layer_norm(): return centred * lax.rsqrt(variance + EPSILON) * norm_gain + norm_bias]
    convert_element_type x30 -> x0, local copies, waits for them, and re-layouts: 46.2 us -> none  [the longest x8 10.3 us: local(): second_flat = second.reshape(-1, second.shape[-1]).astype(jnp.bfloat16)]
    reduce_scatter x4 -> x0, waiting for transfers between devices: 44.9 us -> none  [the longest x2 44.8 us: local(): lax.psum_scatter(band_grads[1].astype(jnp.bfloat16), 'rows', scatter_dime...]
  transfers between devices with their start and end apart: 17 -> 0, of which waited for: 12 -> 0; matrix products, arithmetic and copies ran while one was open for 38% -> 0% of each run, Pallas kernels for 0% -> 0%
where the time goes in v1:
time: 222 us
  Pallas kernels  186 us (84%)
  local copies, waits for them, and re-layouts  23.3 us (10%)
  other arithmetic  10.7 us (5%)
    pallas_call x1, Pallas kernels, backward(): pl.pallas_call(partial(backward_kernel, rows, batch, groups, pair), grid=...  122 us
    pallas_call x1, Pallas kernels, forward(): pl.pallas_call(partial(forward_kernel, rows, groups, pair), grid=(groups...  51.5 us
    unnamed x32, local copies, waits for them, and re-layouts  12.3 us
    pallas_call x1, Pallas kernels, unpack(): pl.pallas_call(unpack_kernel, grid_spec=pltpu.PrefetchScalarGridSpec(num_...  12 us

profile of v1, /device:TPU:0, one launch (start us, length us, event | category | flops | bytes accessed | tf_op | source)
XLA Modules:
  0.0 221.8 jit_solution(1261905950398533978)
XLA Ops:
  0.6 0.0 copy-start.10
  0.7 0.5 and_select_fusion.1.order
  1.2 0.1 pad.5.clone
  1.3 1.3 fusion.18
  2.6 0.7 add_compare_fusion.1
  3.3 0.7 add_compare_fusion
  4.0 0.8 slice_bitcast_fusion.6
  4.8 0.7 add_convert_fusion.live
  5.4 0.8 broadcast_multiply_fusion
  6.2 0.1 eq.46
  6.3 1.3 broadcast_in_dim.83.gain1
  7.5 1.3 broadcast_in_dim.84.gain2
  8.8 0.6 gather_fusion.1
  9.5 0.6 gather_fusion
  10.1 0.6 gather_fusion.3
  10.7 0.6 gather_fusion.2
  11.4 0.8 fusion.9
  12.2 0.9 fusion.5
  13.1 0.1 multiply_bitcast_fusion.1
  13.2 0.1 reshape.400
  13.3 0.7 copy.61.mix
  14.1 0.8 fusion.1.place
  14.9 0.7 fusion.12
  15.6 0.4 fusion
  16.0 0.1 copy.54
  16.1 0.7 reshape.399.filt_s
  16.8 0.5 eq.43
  17.3 0.3 eq.44
  17.6 0.7 compare_convert_fusion.pick
  18.3 1.0 multiply_bitcast_fusion.filt_l
  19.3 0.2 copy.56
  19.5 0.2 reshape.402
  19.7 1.3 copy.59
  21.0 0.2 reshape.404
  21.3 0.1 copy.55
  21.4 0.1 copy.57
  21.6 0.9 copy-done.5
  22.5 0.1 copy.58
  22.6 0.1 copy.60
  22.8 3.0 %maximum_maximum_fusion.1 = (bf16[24,96,384]{2,1,0:T(8,128)(2,1)}, bf16[24,96,384]{2,1,0:T(8,128)(2,1)}) fusion(bf16[24,36,384]{2,1,0:T(8,128)(2,1)S(1)} %reshape.404, bf16[24,56,384]{2,1,0:T(8,128)(2,1)S(1)} %copy.60, bf16[96]{0:T(256)(128)(2,1)S(1)} %pad.5.clone, bf16[24,36,384]{2,1,0:T(8,128)(2,1)S(1)} %reshape.402, bf16[24,56,384]{2,1,0:T(8,128)(2,1)S(1)} %copy.57), kind=kLoop, calls=%fused_computation.5 | loop fusion | flops 9732096 | bytes 6930624 | tf_op jit(solution)/shard_map/concatenate | solution.py:656
  25.8 51.5 %forward.1 = (bf16[4,6,96,384]{3,2,1,0:T(8,128)(2,1)}, f32[2,6,304,384]{3,2,1,0:T(8,128)}, f32[2,6,304,384]{3,2,1,0:T(8,128)}, f32[2,6,368,384]{3,2,1,0:T(8,128)...) custom-call(bf16[24,96,384]{2,1,0:T(8,128)(2,1)} %get-tuple-element., ...), custom_call_target="tpu_custom_call" | custom-call | tf_op jit(solution)/shard_map/forward/pallas_call | solution.py:211
  77.3 122.5 %backward.1 = (bf16[4,6,96,384]{3,2,1,0:T(8,128)(2,1)}, bf16[4,6,96,384]{3,2,1,0:T(8,128)(2,1)}, bf16[9216,256]{1,0:T(8,128)(2,1)}, bf16[512,384]{1,0:T(8,128)(2,1)}) custom-call(f32[6,4]{1,0:T(8,128)} %add_convert_fusion.live, bf16[304,384]{1,0:T(8,128)(2,1)} %compare_convert_fusion.pick, bf16[384,304]{1,0:T(8,128)(2,1)} %fusion.1.place, ...), custom_call_target="tpu_custom_call" | custom-call | tf_op jit(solution)/shard_map/backward/pallas_call | solution.py:532
  199.7 12.0 %unpack.1 = (f32[24,1,4,14,384]{4,3,2,1,0:T(8,128)}, f32[72,1,2,6,384]{4,3,2,1,0:T(8,128)}, f32[24,1,4,14,384]{4,3,2,1,0:T(8,128)}, f32[72,1,2,6,384]{4,3,2,1,0:...) custom-call(s32[4]{0:T(128)} %and_select_fusion.1.order, ...), custom_call_target="tpu_custom_call" | custom-call | tf_op jit(solution)/shard_map/unpack/pallas_call | solution.py:606
  211.7 3.9 %copy.62 = f32[24,1,4,14,384]{4,2,3,1,0:T(4,128)} copy(f32[24,1,4,14,384]{4,3,2,1,0:T(8,128)} %get-tuple-element.68) | data formatting | bytes 4128768
  215.6 0.6 slice_bitcast_fusion
  216.2 1.7 copy.63
  218.0 1.7 copy.65
  219.7 2.1 copy.64
  (28 shorter events, 0.1 us)
Async XLA Ops:
  0.6 15.0 %copy-start.10 = (f32[4]{0:T(128)S(1)}, f32[4]{0:T(128)}, u32[]{:S(2)}) copy-start(f32[4]{0:T(128)} %constant.77) | copy-start | bytes 52
  0.7 14.2 %copy-start = (f32[2,2,14,8,384]{4,3,2,1,0:T(8,128)S(1)}, f32[2,2,14,8,384]{4,3,2,1,0:T(8,128)}, u32[]{:S(2)}) copy-start(f32[2,2,14,8,384]{4,3,2,1,0:T(8,128)} %param.40) | copy-start | bytes 2064388
  0.7 14.2 %copy-start.9 = (f32[4,8]{1,0:T(4,128)S(1)}, f32[4,8]{1,0:T(4,128)}, u32[]{:S(2)}) copy-start(f32[4,8]{1,0:T(4,128)} %param.37) | copy-start | bytes 388
  0.7 12.4 %copy-start.7 = (f32[6,14]{1,0:T(8,128)S(1)}, f32[6,14]{1,0:T(8,128)}, u32[]{:S(2)}) copy-start(f32[6,14]{1,0:T(8,128)} %param.36) | copy-start | bytes 1012
  14.9 3.4 %copy-start.11 = (f32[8]{0:T(128)S(1)}, f32[8]{0:T(128)}, u32[]{:S(2)}) copy-start(f32[8]{0:T(128)} %constant.76) | copy-start | bytes 100
  16.0 3.3 %copy-start.6 = (bf16[72,1,2,6,384]{4,2,3,1,0:T(2,128)(2,1)S(1)}, bf16[72,1,2,6,384]{4,2,3,1,0:T(2,128)(2,1)}, u32[]{:S(2)}) copy-start(bf16[72,1,2,6,384]{4,2,3,1,0:T(2,128)(2,1)} %param.31) | copy-start | bytes 1990660
  19.5 1.8 copy-start.4
  21.3 1.2 copy-start.5
  211.7 3.9 %copy-start.8 = (f32[5,2,384]{2,1,0:T(2,128)S(1)}, f32[5,2,384]{2,1,0:T(2,128)}, u32[]{:S(2)}) copy-start(f32[5,2,384]{2,1,0:T(2,128)} %get-tuple-element.50) | copy-start | bytes 46084
  211.7 4.5 %copy-start.3 = (f32[72,1,2,6,384]{4,3,2,1,0:T(8,128)S(1)}, f32[72,1,2,6,384]{4,3,2,1,0:T(8,128)}, u32[]{:S(2)}) copy-start(f32[72,1,2,6,384]{4,3,2,1,0:T(8,128)} %get-tuple-element.69) | copy-start | bytes 3981316
  215.6 2.4 %copy-start.2 = (f32[72,1,2,6,384]{4,3,2,1,0:T(8,128)S(1)}, f32[72,1,2,6,384]{4,3,2,1,0:T(8,128)}, u32[]{:S(2)}) copy-start(f32[72,1,2,6,384]{4,3,2,1,0:T(8,128)} %get-tuple-element.71) | copy-start | bytes 3981316
  216.2 3.5 %copy-start.1 = (f32[24,1,4,14,384]{4,3,2,1,0:T(8,128)S(1)}, f32[24,1,4,14,384]{4,3,2,1,0:T(8,128)}, u32[]{:S(2)}) copy-start(f32[24,1,4,14,384]{4,3,2,1,0:T(8,128)} %get-tuple-element.70) | copy-start | bytes 6193156

commit v2 on v1

--- a/solution.py
+++ b/solution.py
@@ -23,6 +23,36 @@
 CH = 512
 CB = 512
 SMALL = 512
+PLAN = {
+    (0, 0): [(-3, 0)],
+    (0, 9): [(0, 0), (-3, 1)],
+    (1, 2): [(0, 1), (-3, 2)],
+    (1, 9): [(1, 0)],
+    (2, 0): [(-3, 3)],
+    (2, 2): [(1, 1)],
+    (2, 9): [(0, 2), (2, 0)],
+    (3, 0): [(-3, 4)],
+    (3, 2): [(2, 1)],
+    (3, 9): [(-3, 5)],
+    (4, 0): [(1, 2)],
+    (4, 9): [(0, 3)],
+    (5, 1): [(2, 2)],
+    (6, 1): [(1, 3)],
+    (6, 9): [(0, 4), (3, 0)],
+    (7, 2): [(2, 3), (3, 1)],
+    (7, 9): [(4, 0)],
+    (8, 0): [(1, 4), (0, 5)],
+    (8, 1): [(4, 1)],
+    (8, 9): [(0, 6), (3, 2), (5, 0)],
+    (9, 0): [(2, 4)],
+    (9, 1): [(1, 5), (5, 1), (-2, 0)],
+    (10, 0): [(1, 6), (4, 2)],
+    (10, 1): [(-2, 1)],
+    (10, 9): [(3, 3)],
+    (11, 0): [(2, 5)],
+    (11, 2): [(-2, 2)],
+    (11, 9): [(2, 6), (5, 2), (-1, 0), (4, 3), (-1, 1), (3, 4), (-1, 2), (-2, 3), (5, 3), (3, 5), (4, 4), (-2, 4), (3, 6), (-1, 3), (5, 4), (-2, 5), (4, 5), (4, 6), (-1, 4), (5, 5), (5, 6), (-1, 5), (-1, 6)],
+}
 MESH = pl.DeviceIdType.MESH
 VMEM_LIMIT = 60 * 2**20
 F32, BF16 = jnp.float32, jnp.bfloat16
@@ -97,12 +127,12 @@
     return h * cdf, cdf + h * dens
 
 
-def live_rows(live, group):
+def live_rows(counts, group):
     t = lax.broadcasted_iota(jnp.int32, (T, 1), 0)
-    mask = jnp.where(t < TL, live[group, 0], live[group, PER])
-    for at in range(PER - 1):
-        mask = jnp.where((t >= TL + at * TS) & (t < TL + (at + 1) * TS), live[group, 1 + at], mask)
-    return mask
+    place, limit = jnp.full((T, 1), group), jnp.where(t < TL, counts[0, 0], counts[0, 1])
+    for at in range(PER):
+        place = jnp.where(t >= TL + at * TS, group * PER + at, place)
+    return jnp.where(place < limit, 1.0, 0.0)
 
 
 def whole(shape):
@@ -113,15 +143,16 @@
     return pl.BlockSpec(memory_space=pltpu.SMEM)
 
 
-def forward_kernel(row_count, groups, pair, packed_in, packed_cot, live, pick, place, gain1, bias1, filt_l, filt_s, gain2, bias2,
-                   w1, b1, w2, b2, tl, ts, tlb, tsb, outs, xs, zs, spec, vs, gs, ps, do,
-                   slots, own_sem, send_sem, recv_sem):
+def forward_kernel(row_count, groups, pair, packed_in, packed_cot, counts, bounds, filters, gain1, bias1, gain2, bias2,
+                   w1, b1, w2, b2, tl, ts, tlb, tsb, need, slot, row_interp, col_interp, row_s, row_l, col_s, col_l, fold,
+                   outs, xs, zs, spec, vs, gs, ps, do, place, filt_l, filt_s, mix,
+                   pick, slots, own_sem, send_sem, recv_sem):
     step = pl.program_id(0)
     batch, row = lax.axis_index("batch"), lax.axis_index("rows")
     last = groups // pair - 1
 
     def remote(which, m, g):
-        to = (row + m) % row_count
+        to = lax.rem(row + m, row_count)
         given = (packed_in, packed_cot)[which]
         return pltpu.make_async_remote_copy(
             src_ref=given.at[to * groups + g], dst_ref=slots.at[which, m, g],
@@ -136,7 +167,7 @@
     def _():
         barrier = pltpu.get_barrier_semaphore()
         for m in range(1, row_count):
-            pl.semaphore_signal(barrier, inc=1, device_id=(batch, (row + m) % row_count), device_id_type=MESH)
+            pl.semaphore_signal(barrier, inc=1, device_id=(batch, lax.rem(row + m, row_count)), device_id_type=MESH)
         for which in range(2):
             @pl.loop(0, groups)
             def _(g):
@@ -147,6 +178,25 @@
             def _(g):
                 for m in range(1, row_count):
                     remote(which, m, g).start()
+        for m in range(row_count):
+            band = lax.rem(row + (row_count - m), row_count)
+            large = lax.broadcasted_iota(jnp.int32, (T, BAND), 0) < TL
+            first = jnp.where(large, bounds[0, band], bounds[1, band])
+            size = jnp.where(large, bounds[0, band + 1], bounds[1, band + 1]) - first
+            hit = (need[...] == first) & (slot[...] < size)
+            hit = jnp.where(hit, 1.0, 0.0)
+            pick[:, m * BAND : (m + 1) * BAND] = hit.astype(BF16)
+            place[m * BAND : (m + 1) * BAND, :] = hit.T.astype(BF16)
+        exact = partial(jnp.dot, preferred_element_type=F32, precision=HIGHEST)
+        both = exact(exact(row_s[...], row_interp[...]), row_l[...]) * exact(exact(col_s[...], col_interp[...]), col_l[...])
+        mix[...] = both
+        for n in range(LAYERS):
+            for c in range(2):
+                filt_l[n, c] = filters[n, c] * fold[...]
+                filt_s[n, c] = exact(both, filters[n, c])
+
+    def live(g):
+        return live_rows(counts, row * groups + g)
 
     def take(which, g):
         mine(which, g).wait()
@@ -189,14 +239,14 @@
             total = total + dot(g, w2[n, c : c + CH, :])
         x = [total[j * T : (j + 1) * T] for j in range(pair)]
     for j in range(pair):
-        spread = dot(place[...], (x[j] * live_rows(live, step * pair + j)).astype(BF16)).astype(BF16)
+        spread = dot(place[...], (x[j] * live(step * pair + j)).astype(BF16)).astype(BF16)
         for m in range(row_count):
             outs[m, j] = spread[m * BAND : (m + 1) * BAND]
 
     @pl.when(step == last)
     def _():
         for g in range(groups):
-            do[g] = (take(1, g) * live_rows(live, g)).astype(BF16)
+            do[g] = (take(1, g) * live(g)).astype(BF16)
         for which in range(2):
             @pl.loop(0, groups)
             def _(g):
@@ -204,27 +254,29 @@
                     remote(which, m, g).wait_send()
 
 
-def forward(mesh, groups, pair, packed_in, packed_cot, live, small):
+def forward(mesh, groups, pair, packed_in, packed_cot, counts, bounds, small):
     rows = mesh.shape["rows"]
     sizes = [(T, D, F32), (T, D, F32), (2 * NL + 2 * PER * NS, D, F32), (T, D, BF16), (T, FF, BF16), (T, FF, BF16)]
+    extra = [((groups, T, D), BF16), ((rows * BAND, T), BF16), ((LAYERS, 2, NL, D), F32), ((LAYERS, 2, NS, D), F32), ((NS, NL), F32)]
     hbm = pl.BlockSpec(memory_space=pl.ANY)
     return pl.pallas_call(
         partial(forward_kernel, rows, groups, pair),
         grid=(groups // pair,),
-        in_specs=[hbm, hbm, scalars()] + [whole(a.shape) for a in small],
+        in_specs=[hbm, hbm, scalars(), scalars()] + [whole(a.shape) for a in small],
         out_specs=[pl.BlockSpec((rows, pair, BAND, D), lambda i: (0, i, 0, 0))]
         + [pl.BlockSpec((LAYERS, pair, a, b), lambda i: (0, i, 0, 0)) for a, b, _ in sizes]
-        + [whole((groups, T, D))],
+        + [whole(a) for a, _ in extra],
         out_shape=[jax.ShapeDtypeStruct((rows, groups, BAND, D), BF16)]
         + [jax.ShapeDtypeStruct((LAYERS, groups, a, b), t) for a, b, t in sizes]
-        + [jax.ShapeDtypeStruct((groups, T, D), BF16)],
-        scratch_shapes=[pltpu.VMEM((2, rows, groups, BAND, D), BF16), pltpu.SemaphoreType.DMA((2, groups)),
+        + [jax.ShapeDtypeStruct(a, t) for a, t in extra],
+        scratch_shapes=[pltpu.VMEM((T, rows * BAND), BF16), pltpu.VMEM((2, rows, groups, BAND, D), BF16), pltpu.SemaphoreType.DMA((2, groups)),
                         pltpu.SemaphoreType.DMA((2, rows - 1, groups)), pltpu.SemaphoreType.DMA((2, rows - 1, groups))],
         compiler_params=pltpu.CompilerParams(collective_id=1, has_side_effects=True, vmem_limit_bytes=VMEM_LIMIT),
         name="forward",
-    )(packed_in, packed_cot, live, *small)
-
-
+    )(packed_in, packed_cot, counts, bounds, *small)
+
+
+SPREAD = True
 LOW = 2
 
 
@@ -243,83 +295,84 @@
 
 class Sum:
     def __init__(self, mesh_rows, mesh_batch, acc, full, out, count, bufs, sems, save_sem):
-        self.batch, self.row = lax.axis_index("batch"), lax.axis_index("rows")
-        self.x_n, self.z_n = mesh_rows // 2, mesh_batch // LOW
+        batch, row = lax.axis_index("batch"), lax.axis_index("rows")
         self.acc, self.full, self.out, self.count, self.bufs, self.sems, self.save_sem = acc, full, out, count, bufs, sems, save_sem
-        core, x, z, y = self.row % 2, self.row // 2, self.batch // LOW, self.batch % LOW
         self.size = kinds(mesh_rows, mesh_batch)
-        self.me = [core, y, z * self.x_n + x]
-
-    def other(self, level, step):
-        core, x, z, y = self.row % 2, self.row // 2, self.batch // LOW, self.batch % LOW
-        at = (self.me[level] + step) % self.size[level]
-        if level == 0:
-            return (self.batch, x * 2 + at), at
-        if level == 1:
-            return (z * LOW + at, self.row), at
-        return ((at // self.x_n) * LOW + y, (at % self.x_n) * 2 + core), at
+        self.levels = len(self.size)
+        x_n = mesh_rows // 2
+        core, x, z, y = lax.rem(row, 2), lax.div(row, 2), lax.div(batch, LOW), lax.rem(batch, LOW)
+        self.me = [core, y, z * x_n + x] if SPREAD else [core, y, x, z]
+        self.others, self.offsets, self.counts = [], [0], [count]
+        for level, n in enumerate(self.size):
+            count //= n
+            self.counts.append(count)
+            self.offsets.append(self.offsets[-1] + self.me[level] * count)
+            found = []
+            for step in range(1, n):
+                at = lax.rem(self.me[level] + step, n)
+                device = [(batch, x * 2 + at), (z * LOW + at, row)]
+                device += [(lax.div(at, x_n) * LOW + y, lax.rem(at, x_n) * 2 + core)] if SPREAD else [
+                    (batch, at * 2 + core), (at * LOW + y, row)]
+                found.append((device[level], at))
+            self.others.append(found)
 
     def region(self, part, level):
-        base, count = part * self.count, self.count
-        for i in range(level):
-            count //= self.size[i]
-            base = base + self.me[i] * count
-        return base, count
+        return part * self.count + self.offsets[level], self.counts[level]
 
     def rows(self, base, count):
         return pl.ds(pl.multiple_of(base, 16), count)
 
     def down(self, part, level, step):
         base, count = self.region(part, level)
-        device, at = self.other(level, step)
+        device, at = self.others[level][step - 1]
         chunk = count // self.size[level]
         return pltpu.make_async_remote_copy(
-            src_ref=self.acc.at[self.rows(base + at * chunk, chunk)], dst_ref=self.bufs[level].at[part, step - 1],
-            send_sem=self.sems[level].at[0, part, step - 1], recv_sem=self.sems[level].at[1, part, step - 1],
+            src_ref=self.acc.at[self.rows(base + at * chunk, chunk)], dst_ref=self.bufs[level].at[part, self.rows((step - 1) * chunk, chunk)],
+            send_sem=self.sems[level].at[0, part], recv_sem=self.sems[level].at[1, part],
             device_id=device, device_id_type=MESH)
 
-    def up(self, part, level, step, arriving=False):
+    def up(self, part, level, step):
         base, count = self.region(part, level + 1)
-        device, _ = self.other(level, step)
-        if arriving:
-            low, _ = self.region(part, level)
-            base = low + (self.me[level] - step + self.size[level]) % self.size[level] * count
         rows = self.rows(base, count)
         return pltpu.make_async_remote_copy(
             src_ref=self.full.at[rows], dst_ref=self.full.at[rows],
-            send_sem=self.sems[level].at[2, part, step - 1], recv_sem=self.sems[level].at[3, part, step - 1],
-            device_id=device, device_id_type=MESH)
+            send_sem=self.sems[level].at[2, part], recv_sem=self.sems[level].at[3, part],
+            device_id=self.others[level][step - 1][0], device_id_type=MESH)
+
+    def arrived(self, part, level, sem):
+        every = self.bufs[level].at[part]
+        pltpu.make_async_copy(every, every, self.sems[level].at[sem, part]).wait()
 
     def save(self, part):
         rows = self.rows(part * self.count, self.count)
         return pltpu.make_async_copy(self.full.at[rows], self.out.at[rows], self.save_sem.at[part])
 
     def stage(self, part, k):
-        if 1 <= k <= 3:
+        top = self.levels
+        if 1 <= k <= top:
             level = k - 1
-            for step in range(1, self.size[level]):
-                self.down(part, level, step).wait()
+            self.arrived(part, level, 0)
+            self.arrived(part, level, 1)
             base, count = self.region(part, level + 1)
-            add_rows(self.full if k == 3 else self.acc, self.acc, base,
-                     [self.bufs[level].at[part, s] for s in range(self.size[level] - 1)], count)
-        if k < 3:
+            add_rows(self.full if k == top else self.acc, self.acc, base,
+                     [self.bufs[level].at[part, self.rows(s * count, count)] for s in range(self.size[level] - 1)], count)
+        if k < top:
             for step in range(1, self.size[k]):
                 self.down(part, k, step).start()
-        if k >= 4:
-            level = 6 - k
-            for step in range(1, self.size[level]):
-                self.up(part, level, step).wait_send()
-                self.up(part, level, step, True).wait_recv()
-        if 3 <= k < 6:
-            for step in range(1, self.size[5 - k]):
-                self.up(part, 5 - k, step).start()
-        if k == 6:
+        if k > top:
+            level = 2 * top - k
+            self.arrived(part, level, 2)
+            self.arrived(part, level, 3)
+        if top <= k < 2 * top:
+            for step in range(1, self.size[2 * top - 1 - k]):
+                self.up(part, 2 * top - 1 - k, step).start()
+        if k == 2 * top:
             self.save(part).start()
 
 
 def kinds(mesh_rows, mesh_batch):
-    size = [2, LOW, (mesh_rows // 2) * (mesh_batch // LOW)]
-    return size
+    x_n, z_n = mesh_rows // 2, mesh_batch // LOW
+    return [2, LOW, x_n * z_n] if SPREAD else [2, LOW, x_n, z_n]
 
 
 def columns(mesh_rows, mesh_batch):
@@ -337,11 +390,11 @@
     shapes = [pltpu.VMEM((parts * count, width), BF16)] * 2
     for n in size:
         count //= n
-        shapes.append(pltpu.VMEM((parts, n - 1, count, width), BF16))
-    return shapes + [pltpu.SemaphoreType.DMA((4, parts, n - 1)) for n in size] + [pltpu.SemaphoreType.DMA((parts,))]
-
-
-def backward_kernel(row_count, batch_count, groups, pair, live, pick, place, gain1, filt_l, filt_s, gain2, w1, w2, tl, ts, tlb, tsb,
+        shapes.append(pltpu.VMEM((parts, (n - 1) * count, width), BF16))
+    return shapes + [pltpu.SemaphoreType.DMA((4, parts)) for n in size] + [pltpu.SemaphoreType.DMA((parts,))]
+
+
+def backward_kernel(row_count, batch_count, groups, pair, place, filt_l, filt_s, gain1, gain2, w1, w2, tl, ts, tlb, tsb,
                     mix, fold, outs, do_in, xs, zs, spec, vs, gs, ps,
                     out_land, grad_land, weights_out, small_out,
                     dx, dv, do, dot_, vt, dh, gslots, dvec, dhid, dfl, dfs, out_sem, grad_sem, own_sem, *sums):
@@ -354,35 +407,67 @@
     width = columns(row_count, batch_count)
     part_rows = padded(row_count, batch_count, 2 * D * (CB // width))
     small_rows = padded(row_count, batch_count, SMALL)
-    weights = Sum(row_count, batch_count, sums[0], sums[1], weights_out, part_rows, sums[2:5], sums[5:8], sums[8])
-    small = Sum(row_count, batch_count, sums[9], sums[10], small_out, small_rows, sums[11:14], sums[14:17], sums[17])
+    sums_of = []
+    for out, count in ((weights_out, part_rows), (small_out, small_rows)):
+        n = len(kinds(row_count, batch_count))
+        sums_of.append(Sum(row_count, batch_count, sums[0], sums[1], out, count, sums[2 : 2 + n], sums[2 + n : 2 + 2 * n], sums[2 + 2 * n]))
+        sums = sums[3 + 2 * n :]
+    weights, small = sums_of
 
     def send_out(m, g):
         return pltpu.make_async_remote_copy(
             src_ref=outs.at[m, g], dst_ref=out_land.at[m, g], send_sem=out_sem.at[0, m - 1, g], recv_sem=out_sem.at[1, m - 1, g],
-            device_id=(batch, (row - m + row_count) % row_count), device_id_type=MESH)
+            device_id=(batch, lax.rem(row + (row_count - m), row_count)), device_id_type=MESH)
 
     def send_grad(m, g):
         return pltpu.make_async_remote_copy(
             src_ref=gslots.at[m, g], dst_ref=grad_land.at[m, g], send_sem=grad_sem.at[0, m - 1, g], recv_sem=grad_sem.at[1, m - 1, g],
-            device_id=(batch, (row - m + row_count) % row_count), device_id_type=MESH)
+            device_id=(batch, lax.rem(row + (row_count - m), row_count)), device_id_type=MESH)
 
     def keep_out():
         return pltpu.make_async_copy(outs.at[0], out_land.at[0], own_sem.at[0])
 
     def keep_grad():
         return pltpu.make_async_copy(gslots.at[0], grad_land.at[0], own_sem.at[1])
+
+    plan = {key: [a for a in PLAN[key] if a[0] != -2 or groups == 6] for key in PLAN}
+    if groups != 6:
+        plan[compute_steps - 1, 9] = [(-2, g) for g in range(groups)] + plan[compute_steps - 1, 9]
+    left = set(plan)
+
+    def do_now(part, k):
+        if part >= 0:
+            weights.stage(part, k)
+        elif part == -1:
+            small.stage(0, k)
+        elif k < groups:
+            for m in range(1, row_count):
+                (send_grad if part == -2 else send_out)(m, k).start()
+
+    def advance(place, steps):
+        for at in steps:
+            found = sorted(key for key in left if key[0] == at and (key[1] == place or place == 9))
+            if found:
+                @pl.when(i == at)
+                def _():
+                    for key in found:
+                        left.discard(key)
+                        for part, k in plan[key]:
+                            do_now(part, k)
+
+    first_steps = [at for at in range(compute_steps) if at % per < chunks]
+    second_steps = [at for at in range(compute_steps) if at % per >= chunks]
 
     @pl.when(i == 0)
     def _():
         barrier = pltpu.get_barrier_semaphore()
         greeted = 0
         for m in range(1, row_count):
-            pl.semaphore_signal(barrier, inc=1, device_id=(batch, (row + m) % row_count), device_id_type=MESH)
+            pl.semaphore_signal(barrier, inc=1, device_id=(batch, lax.rem(row + m, row_count)), device_id_type=MESH)
             greeted += 1
-        for level in (1, 2):
+        for level in range(1, weights.levels):
             for step in range(1, weights.size[level]):
-                pl.semaphore_signal(barrier, inc=1, device_id=weights.other(level, step)[0], device_id_type=MESH)
+                pl.semaphore_signal(barrier, inc=1, device_id=weights.others[level][step - 1][0], device_id_type=MESH)
                 greeted += 1
         keep_out().start()
         if part_rows > 2 * D * (CB // width):
@@ -393,11 +478,6 @@
             ref[...] = jnp.zeros_like(ref)
         pl.semaphore_wait(barrier, greeted)
 
-    @pl.when(i < groups)
-    def _():
-        for m in range(1, row_count):
-            send_out(m, i).start()
-
     @pl.when((i < compute_steps) & (q == 0))
     def _():
         for g in range(groups):
@@ -419,6 +499,7 @@
             part = (dot_nt(some, w2[0]) * slope.astype(F32)).astype(BF16)
             dh[rows] = part
             dv[g : g + pair] += dot_nt(part, w1[0]).reshape(pair, T, D)
+            advance(g // pair, first_steps)
         part = (LAYERS - 1 - layer) * chunks + q
         base = part * part_rows
         one = dot(vt[...], dh[...])
@@ -432,19 +513,22 @@
     @pl.when((i < compute_steps) & (q >= chunks))
     def _():
         for j in range(pair):
+            if j:
+                advance(2 * j - 1, second_steps)
             g = (q - chunks) * pair + j
             dvg = dv[g]
             u, scale = normal(zs[0, j])
             row_sum = lambda a: jnp.sum(a, axis=0, keepdims=True)
             dvec[layer, 2:3] += row_sum(dvg * u)
             dvec[layer, 3:4] += row_sum(dvg)
-            dz = normal_back(dvg, gain2[0], u, scale).astype(BF16)
+            dz = normal_back(dvg, gain2[pl.ds(layer, 1)], u, scale).astype(BF16)
             yl, ysm = analyse(tl[...], ts[...], dz)
             lr, li = yl[:NL], yl[NL:]
             sr, si = ysm[: PER * NS], ysm[PER * NS :]
             xr, xi = spec[0, j, :NL], spec[0, j, NL : 2 * NL]
             dfl[layer, :NL] += lr * xr + li * xi
             dfl[layer, NL:] += li * xr - lr * xi
+            advance(2 * j, second_steps)
             gr, gi = filt_l[0, 0], filt_l[0, 1]
             dl = jnp.concatenate([lr * gr + li * gi, li * gr - lr * gi], axis=0).astype(BF16)
             xr, xi = spec[0, j, 2 * NL : 2 * NL + PER * NS], spec[0, j, 2 * NL + PER * NS :]
@@ -457,7 +541,7 @@
             u, scale = normal(xs[0, j])
             dvec[layer, 0:1] += row_sum(du * u)
             dvec[layer, 1:2] += row_sum(du)
-            grad = dx[g] + normal_back(du, gain1[0], u, scale)
+            grad = dx[g] + normal_back(du, gain1[pl.ds(layer, 1)], u, scale)
             dx[g] = grad
 
             @pl.when(layer == 0)
@@ -465,18 +549,17 @@
                 spread = dot(place[...], grad.astype(BF16)).astype(BF16)
                 for m in range(row_count):
                     gslots[m, g] = spread[m * BAND : (m + 1) * BAND]
-                for m in range(1, row_count):
-                    send_grad(m, g).start()
 
     @pl.when(i == compute_steps - 1)
     def _():
         small.acc[...] = jnp.zeros_like(small.acc)
         exact = partial(jnp.dot, preferred_element_type=F32, precision=HIGHEST)
+        mix_t = mix[...].T
         for n in range(LAYERS):
             for c in range(2):
                 at = (n * 2 + c) * NL
                 small.acc[at : at + NL, :] = (dfl[n, c * NL : (c + 1) * NL] * fold[...]
-                                              + exact(mix[...], dfs[n, c * NS : (c + 1) * NS])).astype(BF16)
+                                              + exact(mix_t, dfs[n, c * NS : (c + 1) * NS])).astype(BF16)
         at = LAYERS * 2 * NL
         rest = [dvec[n, k : k + 1] for n in range(LAYERS) for k in range(5)]
         rest += [dhid[n, :, c : c + D] for n in range(LAYERS) for c in range(0, FF, D)]
@@ -485,16 +568,7 @@
         small.acc[at : at + rest.shape[0], :] = rest
         keep_grad().start()
 
-    for k in range(6, -1, -1):
-        made = i - k
-
-        @pl.when((made >= 0) & (made < compute_steps) & (made % per < chunks))
-        def _():
-            weights.stage(made // per * chunks + made % per, k)
-
-        @pl.when(made == compute_steps - 1)
-        def _():
-            small.stage(0, k)
+    advance(9, range(compute_steps))
 
     @pl.when(i == pl.num_programs(0) - 1)
     def _():
@@ -510,12 +584,12 @@
         small.save(0).wait()
 
 
-def backward(mesh, groups, pair, live, small, tabs, mix, fold, outs, do, saved):
+def backward(mesh, groups, pair, small, tabs, mix, fold, outs, do, saved):
     rows, batch = mesh.shape["rows"], mesh.shape["batch"]
-    pick, place, gain1, filt_l, filt_s, gain2, w1, w2 = small
+    place, filt_l, filt_s, gain1, gain2, w1, w2 = small
     chunks, pairs = FF // CB, groups // pair
     per, last = chunks + pairs, LAYERS - 1
-    steps = LAYERS * per + 6
+    steps = LAYERS * per
     layer = lambda i: jnp.maximum(last - i // per, 0)
     when = lambda i: jnp.where(i < LAYERS * per, i % per, per - 1)
     chunk = lambda i: jnp.minimum(when(i), chunks - 1)
@@ -523,7 +597,6 @@
     per_layer = lambda a: pl.BlockSpec((1,) + a.shape[1:], lambda i: (layer(i),) + (0,) * (a.ndim - 1))
     by_pair = lambda a: pl.BlockSpec((1, pair) + a.shape[2:], lambda i: (layer(i), place_of(i), 0, 0))
     by_chunk = lambda a: pl.BlockSpec((1, groups, T, CB), lambda i: (layer(i), 0, 0, chunk(i)))
-    gain1, gain2 = gain1[:, None], gain2[:, None]
     xs, zs, spec, vs, gs, ps = saved
     hbm = pl.BlockSpec(memory_space=pl.ANY)
     width = columns(rows, batch)
@@ -532,7 +605,7 @@
     return pl.pallas_call(
         partial(backward_kernel, rows, batch, groups, pair),
         grid=(steps,),
-        in_specs=[scalars(), whole(pick.shape), whole(place.shape)] + [per_layer(a) for a in (gain1, filt_l, filt_s, gain2)]
+        in_specs=[whole(place.shape), per_layer(filt_l), per_layer(filt_s), whole(gain1.shape), whole(gain2.shape)]
         + [pl.BlockSpec((1, D, CB), lambda i: (layer(i), 0, chunk(i))), pl.BlockSpec((1, CB, D), lambda i: (layer(i), chunk(i), 0))]
         + [whole(a.shape) for a in (*tabs, mix, fold)] + [hbm, whole(do.shape)]
         + [by_pair(xs), by_pair(zs), by_pair(spec), per_layer(vs), by_chunk(gs), by_chunk(ps)],
@@ -548,7 +621,7 @@
         + sum_scratch(rows, batch, LAYERS * chunks, part_rows, width) + sum_scratch(rows, batch, 1, small_rows, D),
         compiler_params=pltpu.CompilerParams(collective_id=2, has_side_effects=True, vmem_limit_bytes=VMEM_LIMIT),
         name="backward",
-    )(live, pick, place, gain1, filt_l, filt_s, gain2, w1, w2, *tabs, mix, fold, outs, do, xs, zs, spec, vs, gs, ps)
+    )(place, filt_l, filt_s, gain1, gain2, w1, w2, *tabs, mix, fold, outs, do, xs, zs, spec, vs, gs, ps)
 
 
 def unpack_kernel(order, outs, grads, weights, small, large_out, small_crops, large_grad, small_grad, dw1, dw2,
@@ -557,12 +630,12 @@
     for given, large, little in ((outs, large_out, small_crops), (grads, large_grad, small_grad)):
         for g in range(given.shape[1]):
             block = given[0, g].astype(F32)
-            for s in range(BL):
-                large[g, 0, s] = block[s * WL : (s + 1) * WL]
+            for s in range(WL):
+                large[g, 0, s] = block[s * BL : (s + 1) * BL]
             for p in range(PER):
-                for s in range(BS):
-                    at = BL * WL + (p * BS + s) * WS
-                    little[g * PER + p, 0, s] = block[at : at + WS]
+                for s in range(WS):
+                    at = BL * WL + (p * WS + s) * BS
+                    little[g * PER + p, 0, s] = block[at : at + BS]
     width = weights.shape[1]
     parts = CB // width
     for c in range(parts):
@@ -597,11 +670,11 @@
     part = lambda i: jnp.minimum(i, parts - 1)
     part_rows = weights.shape[0] // parts
     given = pl.BlockSpec((1, groups, BAND, D), lambda i, order: (order[dev(i)], 0, 0, 0))
-    large = pl.BlockSpec((groups, 1, BL, WL, D), lambda i, order: (dev(i), 0, 0, 0, 0))
-    little = pl.BlockSpec((groups * PER, 1, BS, WS, D), lambda i, order: (dev(i), 0, 0, 0, 0))
+    large = pl.BlockSpec((groups, 1, WL, BL, D), lambda i, order: (dev(i), 0, 0, 0, 0))
+    little = pl.BlockSpec((groups * PER, 1, WS, BS, D), lambda i, order: (dev(i), 0, 0, 0, 0))
     every = lambda shape: pl.BlockSpec(shape, lambda i, order: (0,) * len(shape))
-    large_shape = jax.ShapeDtypeStruct((crops, 1, BL, WL, D), F32)
-    little_shape = jax.ShapeDtypeStruct((crops * PER, 1, BS, WS, D), F32)
+    large_shape = jax.ShapeDtypeStruct((crops, 1, WL, BL, D), F32)
+    little_shape = jax.ShapeDtypeStruct((crops * PER, 1, WS, BS, D), F32)
     shapes = [(LAYERS, 2, NL, D), (5, LAYERS, D), (LAYERS, FF)]
     return pl.pallas_call(
         unpack_kernel,
@@ -620,20 +693,26 @@
     )(order, outs, grads, weights, small)
 
 
-def token_columns(rows, band_bounds, me):
-    t = np.arange(T)
-    small = t >= TL
-    at = np.where(small, (t - TL) % TS, t)
-    wide = np.where(small, WS, WL)
-    r, w = jnp.asarray(at // wide, jnp.int32), at % wide
-    crop = np.where(small, (t - TL) // TS, 0)
-    start = jnp.asarray(np.where(small, BL * WL + crop * BS * WS + w, w), jnp.int32)
-    band = (me - jnp.arange(rows, dtype=jnp.int32)) % rows
-    first, end = jnp.where(small[:, None], band_bounds[1][band], band_bounds[0][band]), jnp.where(
-        small[:, None], band_bounds[1][band + 1], band_bounds[0][band + 1])
-    inside = (r[:, None] >= first) & (r[:, None] < end)
-    column = start[:, None] + (r[:, None] - first) * jnp.asarray(wide, jnp.int32)[:, None]
-    return jnp.where(inside, column, -1)
+def wanted_rows():
+    t, c = np.arange(T), np.arange(BAND)
+    small_t, small_c = t >= TL, c >= BL * WL
+    at = np.where(small_t, (t - TL) % TS, t)
+    wide = np.where(small_t, WS, WL)
+    r, w, crop = at // wide, at % wide, np.where(small_t, (t - TL) // TS, 0)
+    at_c = np.where(small_c, (c - BL * WL) % (BS * WS), c)
+    slots = np.where(small_c, BS, BL)
+    s_c, w_c, crop_c = at_c % slots, at_c // slots, np.where(small_c, (c - BL * WL) // (BS * WS), 0)
+    same = (small_t[:, None] == small_c) & (w[:, None] == w_c) & (crop[:, None] == crop_c)
+    return np.where(same, r[:, None] - s_c, -99).astype(np.int32), s_c[None].astype(np.int32)
+
+
+def interp_tables():
+    fold_l = np.where((np.arange(FL) == 0) | (2 * np.arange(FL) == WL), 1.0, 2.0)
+    fold_s = np.where((np.arange(FS) == 0) | (2 * np.arange(FS) == WS), 1.0, 2.0)
+    each = lambda n, times: np.repeat(np.eye(n), times, axis=0)
+    again = lambda n, times: np.tile(np.eye(n), (times, 1))
+    return [jnp.asarray(a, F32) for a in (each(HS, FS), each(HL, FL).T, again(FS, HS) * np.tile(fold_s, HS)[:, None],
+                                          again(FL, HL).T, np.tile(fold_l, HL)[:, None])]
 
 
 def local(mesh, large_in, small_in, large_cot, small_cot, crop_counts, band_bounds, row_interp, col_interp,
@@ -644,35 +723,26 @@
     groups = crops // rows
     pair = 2 if groups % 2 == 0 else 1
     tabs = tables()
-    column = token_columns(rows, band_bounds, me)
-    pick = (column[:, :, None] == jnp.arange(BAND, dtype=jnp.int32)).astype(BF16).reshape(T, rows * BAND)
-    place = (column.T[:, None, :] == jnp.arange(BAND, dtype=jnp.int32)[None, :, None]).astype(BF16).reshape(rows * BAND, T)
-    at = me * groups + jnp.arange(groups, dtype=jnp.int32)
-    live = jnp.concatenate([(at < crop_counts[0, 0])[:, None],
-                            (at[:, None] * PER + jnp.arange(PER, dtype=jnp.int32)) < crop_counts[0, 1]], axis=1)
-    live = live.astype(F32)
+    filters = filters.reshape(LAYERS, 2, NL, D)
 
     def pack(large, small):
-        return jnp.concatenate([large.reshape(crops, BL * WL, D), small.reshape(crops, PER * BS * WS, D),
+        return jnp.concatenate([large.transpose(0, 1, 3, 2, 4).reshape(crops, BL * WL, D),
+                                small.transpose(0, 1, 3, 2, 4).reshape(crops, PER * BS * WS, D),
                                 jnp.zeros((crops, BAND - BL * WL - PER * BS * WS, D), large.dtype)], axis=1)
 
-    small_filter = jnp.einsum("ka,ncabd,lb->nckld", row_interp, filters, col_interp, precision=HIGHEST)
-    fold_l = np.where((np.arange(FL) == 0) | (2 * np.arange(FL) == WL), 1.0, 2.0).astype(np.float32)
-    fold_s = np.where((np.arange(FS) == 0) | (2 * np.arange(FS) == WS), 1.0, 2.0).astype(np.float32)
-    filt_l = (filters * fold_l[:, None]).reshape(LAYERS, 2, NL, D)
-    filt_s = (small_filter * fold_s[:, None]).reshape(LAYERS, 2, NS, D)
-    mix = jnp.einsum("ka,lb->abkl", row_interp, col_interp * fold_s[:, None]).reshape(NL, NS)
-    fold = jnp.asarray(np.tile(fold_l, HL)[:, None])
-
-    outs, *saved, do = forward(mesh, groups, pair, pack(large_in, small_in), pack(large_cot, small_cot), live,
-                               (pick, place, norm1_gain, norm1_bias, filt_l, filt_s, norm2_gain, norm2_bias,
-                                fc1_weight, fc1_bias, fc2_weight, fc2_bias, *tabs))
+    need, slot = wanted_rows()
+    extras = (jnp.asarray(need), jnp.asarray(slot), row_interp, col_interp, *interp_tables())
+    outs, *saved, do, place, filt_l, filt_s, mix = forward(mesh, groups, pair, pack(large_in, small_in), pack(large_cot, small_cot), crop_counts, band_bounds,
+                               (filters, norm1_gain, norm1_bias, norm2_gain, norm2_bias, fc1_weight, fc1_bias, fc2_weight, fc2_bias,
+                                *tabs, *extras))
     outs, grads, weights, small = backward(
-        mesh, groups, pair, live, (pick, place, norm1_gain, filt_l, filt_s, norm2_gain, fc1_weight, fc2_weight), tabs,
-        mix, fold, outs, do, saved)
+        mesh, groups, pair, (place, filt_l, filt_s, norm1_gain, norm2_gain, fc1_weight, fc2_weight), tabs,
+        mix, extras[-1], outs, do, saved)
     large_out, small_out, large_grad, small_grad, dw1, dw2, dfilter, dvec, dhid = unpack(
         mesh, groups, outs, grads, weights, small)
-    return (large_out, small_out, large_grad, small_grad, dvec[0], dvec[1], dfilter.reshape(filters.shape), dvec[2], dvec[3],
+    large_out, small_out, large_grad, small_grad = (
+        a.transpose(0, 1, 3, 2, 4) for a in (large_out, small_out, large_grad, small_grad))
+    return (large_out, small_out, large_grad, small_grad, dvec[0], dvec[1], dfilter.reshape(LAYERS, 2, HL, FL, D), dvec[2], dvec[3],
             dw1, dhid, dw2, dvec[4])
 
 

time: 222 us -> 173 us (0.78)
  Pallas kernels: 186 us -> 160 us
  local copies, waits for them, and re-layouts: 23.3 us -> 7.58 us
  other arithmetic: 10.7 us -> 3.51 us
    pallas_call x1, Pallas kernels: 122 us -> 96.9 us  [backward(): pl.pallas_call(partial(backward_kernel, rows, batch, groups, pair), grid=...]
    unnamed x32 -> x2, local copies, waits for them, and re-layouts: 12.3 us -> 0.01 us
    reshape x7 -> x4, local copies, waits for them, and re-layouts: 2.25 us -> 6.2 us  [the longest x2 4.17 us: pack(): small.transpose(0, 1, 3, 2, 4).reshape(crops, PER * BS * WS, D)]
    gather x4 -> x0, local copies, waits for them, and re-layouts: 2.56 us -> none  [the longest x1 0.64 us: token_columns(): band_bounds[0][band + 1]]
    broadcast_in_dim x2 -> x0, local copies, waits for them, and re-layouts: 2.53 us -> none  [backward(): gain1, gain2 = (gain1[:, None], gain2[:, None])]
    convert_element_type x3 -> x0, other arithmetic: 2.23 us -> none  [the longest x1 0.83 us: local(): (column.T[:, None, :] == jnp.arange(BAND, dtype=jnp.int32)[None, :, None]...]
where the time goes in v2:
time: 173 us; the launch traced here: 172 us
  Pallas kernels  160 us (92%)
  local copies, waits for them, and re-layouts  7.58 us (4%)
  other arithmetic  3.51 us (2%)
    pallas_call x1, Pallas kernels, backward(): pl.pallas_call(partial(backward_kernel, rows, batch, groups, pair), grid=...  96.9 us
    pallas_call x1, Pallas kernels, forward(): pl.pallas_call(partial(forward_kernel, rows, groups, pair), grid=(groups...  51.9 us
    pallas_call x1, Pallas kernels, unpack(): pl.pallas_call(unpack_kernel, grid_spec=pltpu.PrefetchScalarGridSpec(num_...  11.7 us
    reshape x2, local copies, waits for them, and re-layouts, pack(): small.transpose(0, 1, 3, 2, 4).reshape(crops, PER * BS * WS, D)  4.17 us

profile of v2, /device:TPU:0, one launch (start us, length us, event | category | flops | bytes accessed | tf_op | source)
XLA Modules:
  0.0 172.3 jit_solution(18283074224345144832)
XLA Ops:
  0.6 0.0 copy-start
  0.7 1.8 %reshape.44 = bf16[24,56,384]{2,1,0:T(8,128)(2,1)S(1)} reshape(bf16[24,1,14,4,384]{4,3,2,1,0:T(4,128)(2,1)} %bitcast.20) | data formatting | bytes 2064384 | tf_op jit(solution)/shard_map/reshape | solution.py:729
  2.5 0.0 copy-done
  2.5 0.2 reshape.46
  2.7 2.1 %reshape.45 = bf16[24,36,384]{2,1,0:T(8,128)(2,1)S(1)} reshape(bf16[72,1,6,2,384]{4,3,2,1,0:T(2,128)(2,1)} %bitcast.23) | data formatting | bytes 1327104 | tf_op jit(solution)/shard_map/reshape | solution.py:730
  4.8 2.1 %reshape.47 = bf16[24,36,384]{2,1,0:T(8,128)(2,1)S(1)} reshape(bf16[72,1,6,2,384]{4,3,2,1,0:T(2,128)(2,1)} %bitcast.24) | data formatting | bytes 1327104 | tf_op jit(solution)/shard_map/reshape | solution.py:730
  6.9 0.1 pad.5.clone
  7.0 3.0 %maximum_maximum_fusion.1 = (bf16[24,96,384]{2,1,0:T(8,128)(2,1)}, bf16[24,96,384]{2,1,0:T(8,128)(2,1)}) fusion(bf16[24,36,384]{2,1,0:T(8,128)(2,1)S(1)} %reshape.47, bf16[24,56,384]{2,1,0:T(8,128)(2,1)S(1)} %reshape.46, bf16[96]{0:T(256)(128)(2,1)S(1)} %pad.5.clone, bf16[24,36,384]{2,1,0:T(8,128)(2,1)S(1)} %reshape.45, bf16[24,56,384]{2,1,0:T(8,128)(2,1)S(1)} %reshape.44), kind=kLoop, calls=%fused_computation.1 | loop fusion | flops 9732096 | bytes 6930624 | tf_op jit(solution)/shard_map/concatenate | solution.py:729
  10.0 51.9 %forward.1 = (bf16[4,6,96,384]{3,2,1,0:T(8,128)(2,1)}, f32[2,6,304,384]{3,2,1,0:T(8,128)}, f32[2,6,304,384]{3,2,1,0:T(8,128)}, f32[2,6,368,384]{3,2,1,0:T(8,128)...) custom-call(bf16[24,96,384]{2,1,0:T(8,128)(2,1)} %get-tuple-element., ...), custom_call_target="tpu_custom_call" | custom-call | tf_op jit(solution)/shard_map/forward/pallas_call | solution.py:262
  61.8 96.9 %backward.1 = (bf16[4,6,96,384]{3,2,1,0:T(8,128)(2,1)}, bf16[4,6,96,384]{3,2,1,0:T(8,128)(2,1)}, bf16[9216,256]{1,0:T(8,128)(2,1)}, bf16[512,384]{1,0:T(8,128)(2,1)}) custom-call(bf16[384,304]{1,0:T(8,128)(2,1)} %get-tuple-element.38.place, f32[2,2,112,384]{3,2,1,0:T(8,128)} %get-tuple-element.39.filt_l, f32[2,2,24,384]{3,2,1,0:T(8,128)} %get-tuple-element.40.filt_s, ...), custom_call_target="tpu_custom_call" | custom-call | tf_op jit(solution)/shard_map/backward/pallas_call | solution.py:605
  158.8 0.5 and_select_fusion.order
  159.3 11.7 %unpack.1 = (f32[24,1,14,4,384]{4,3,2,1,0:T(4,128)}, f32[72,1,6,2,384]{4,3,2,1,0:T(2,128)}, f32[24,1,14,4,384]{4,3,2,1,0:T(4,128)}, f32[72,1,6,2,384]{4,3,2,1,0:...) custom-call(s32[4]{0:T(128)} %and_select_fusion.order, ...), custom_call_target="tpu_custom_call" | custom-call | tf_op jit(solution)/shard_map/unpack/pallas_call | solution.py:679
  171.0 1.3 slice_bitcast_fusion
  (1 shorter events, 0.0 us)
Async XLA Ops:
  0.6 1.8 %copy-start = (bf16[24,1,4,14,384]{4,2,3,1,0:T(4,128)(2,1)S(1)}, bf16[24,1,4,14,384]{4,2,3,1,0:T(4,128)(2,1)}, u32[]{:S(2)}) copy-start(bf16[24,1,4,14,384]{4,2,3,1,0:T(4,128)(2,1)} %param.30) | copy-start | bytes 3096580

commit v3 on v2

--- a/solution.py
+++ b/solution.py
@@ -33,25 +33,23 @@
     (2, 9): [(0, 2), (2, 0)],
     (3, 0): [(-3, 4)],
     (3, 2): [(2, 1)],
-    (3, 9): [(-3, 5)],
-    (4, 0): [(1, 2)],
-    (4, 9): [(0, 3)],
-    (5, 1): [(2, 2)],
-    (6, 1): [(1, 3)],
-    (6, 9): [(0, 4), (3, 0)],
-    (7, 2): [(2, 3), (3, 1)],
-    (7, 9): [(4, 0)],
-    (8, 0): [(1, 4), (0, 5)],
-    (8, 1): [(4, 1)],
-    (8, 9): [(0, 6), (3, 2), (5, 0)],
-    (9, 0): [(2, 4)],
-    (9, 1): [(1, 5), (5, 1), (-2, 0)],
-    (10, 0): [(1, 6), (4, 2)],
-    (10, 1): [(-2, 1)],
-    (10, 9): [(3, 3)],
-    (11, 0): [(2, 5)],
-    (11, 2): [(-2, 2)],
-    (11, 9): [(2, 6), (5, 2), (-1, 0), (4, 3), (-1, 1), (3, 4), (-1, 2), (-2, 3), (5, 3), (3, 5), (4, 4), (-2, 4), (3, 6), (-1, 3), (5, 4), (-2, 5), (4, 5), (4, 6), (-1, 4), (5, 5), (5, 6), (-1, 5), (-1, 6)],
+    (4, 0): [(-3, 5)],
+    (4, 1): [(1, 2)],
+    (5, 1): [(0, 3)],
+    (5, 2): [(2, 2)],
+    (6, 9): [(1, 3), (3, 0)],
+    (7, 1): [(0, 4)],
+    (7, 2): [(3, 1)],
+    (7, 9): [(4, 0), (2, 3)],
+    (8, 2): [(4, 1)],
+    (8, 9): [(1, 4), (0, 5), (5, 0)],
+    (9, 1): [(3, 2)],
+    (9, 2): [(0, 6)],
+    (9, 9): [(5, 1), (2, 4), (-2, 0)],
+    (10, 1): [(4, 2)],
+    (11, 0): [(-2, 1)],
+    (11, 1): [(1, 5)],
+    (11, 9): [(3, 3), (-1, 0), (1, 6), (5, 2), (-1, 1), (4, 3), (2, 5), (-1, 2), (2, 6), (3, 4), (-2, 2), (5, 3), (3, 5), (-2, 3), (4, 4), (3, 6), (-1, 3), (5, 4), (-2, 4), (4, 5), (-1, 4), (-2, 5), (4, 6), (5, 5), (-1, 5), (5, 6), (-1, 6)],
 }
 MESH = pl.DeviceIdType.MESH
 VMEM_LIMIT = 60 * 2**20
@@ -143,25 +141,29 @@
     return pl.BlockSpec(memory_space=pltpu.SMEM)
 
 
-def forward_kernel(row_count, groups, pair, packed_in, packed_cot, counts, bounds, filters, gain1, bias1, gain2, bias2,
+def forward_kernel(row_count, groups, pair, large_in, small_in, large_cot, small_cot, counts, bounds, filters, gain1, bias1, gain2, bias2,
                    w1, b1, w2, b2, tl, ts, tlb, tsb, need, slot, row_interp, col_interp, row_s, row_l, col_s, col_l, fold,
-                   outs, xs, zs, spec, vs, gs, ps, do, place, filt_l, filt_s, mix,
-                   pick, slots, own_sem, send_sem, recv_sem):
+                   outs, xs, zs, both_scales, spec, vs, gs, ps, do, place, filt_l, filt_s, mix,
+                   pick, lined, large_slots, small_slots, own_sem, send_sem, recv_sem):
     step = pl.program_id(0)
     batch, row = lax.axis_index("batch"), lax.axis_index("rows")
     last = groups // pair - 1
 
+    def ends(which, m, g, to):
+        crop = to * groups + g
+        return (((large_in, large_cot)[which].at[crop, 0], large_slots.at[which, m, g]),
+                ((small_in, small_cot)[which].at[pl.ds(crop * PER, PER), 0], small_slots.at[which, m, g]))
+
     def remote(which, m, g):
         to = lax.rem(row + m, row_count)
-        given = (packed_in, packed_cot)[which]
-        return pltpu.make_async_remote_copy(
-            src_ref=given.at[to * groups + g], dst_ref=slots.at[which, m, g],
-            send_sem=send_sem.at[which, m - 1, g], recv_sem=recv_sem.at[which, m - 1, g],
-            device_id=(batch, to), device_id_type=MESH)
+        return [pltpu.make_async_remote_copy(
+            src_ref=source, dst_ref=target,
+            send_sem=send_sem.at[which, k, m - 1, g], recv_sem=recv_sem.at[which, k, m - 1, g],
+            device_id=(batch, to), device_id_type=MESH) for k, (source, target) in enumerate(ends(which, m, g, to))]
 
     def mine(which, g):
-        given = (packed_in, packed_cot)[which]
-        return pltpu.make_async_copy(given.at[row * groups + g], slots.at[which, 0, g], own_sem.at[which, g])
+        return [pltpu.make_async_copy(source, target, own_sem.at[which, k, g])
+                for k, (source, target) in enumerate(ends(which, 0, g, row))]
 
     @pl.when(step == 0)
     def _():
@@ -171,13 +173,16 @@
         for which in range(2):
             @pl.loop(0, groups)
             def _(g):
-                mine(which, g).start()
+                for copy in mine(which, g):
+                    copy.start()
         pl.semaphore_wait(barrier, row_count - 1)
         for which in range(2):
             @pl.loop(0, groups)
             def _(g):
                 for m in range(1, row_count):
-                    remote(which, m, g).start()
+                    for copy in remote(which, m, g):
+                        copy.start()
+        lined[...] = jnp.zeros_like(lined)
         for m in range(row_count):
             band = lax.rem(row + (row_count - m), row_count)
             large = lax.broadcasted_iota(jnp.int32, (T, BAND), 0) < TL
@@ -199,33 +204,51 @@
         return live_rows(counts, row * groups + g)
 
     def take(which, g):
-        mine(which, g).wait()
+        for copy in mine(which, g):
+            copy.wait()
         for m in range(1, row_count):
-            remote(which, m, g).wait_recv()
-        return dot(pick[...], jnp.concatenate([slots[which, m, g] for m in range(row_count)], axis=0))
-
+            for copy in remote(which, m, g):
+                copy.wait_recv()
+        for m in range(row_count):
+            at = m * BAND
+            for w in range(WL):
+                lined[at + w * BL : at + (w + 1) * BL, :] = large_slots[which, m, g, w].astype(F32)
+            at += BL * WL
+            for p in range(PER):
+                for w in range(WS):
+                    row_at = at + (p * WS + w) * BS
+                    lined[row_at : row_at + BS, :] = small_slots[which, m, g, p, w].astype(F32)
+        return dot(pick[...], lined[...].astype(BF16))
+
+    side = lambda parts: jnp.concatenate(parts, axis=1)
+    lanes = lambda a: [a[:, j * D : (j + 1) * D] for j in range(pair)]
     x = [take(0, step * pair + j) for j in range(pair)]
     for n in range(LAYERS):
+        u, scales = [], []
+        for j in range(pair):
+            unit, scale = normal(x[j])
+            xs[n, j] = unit.astype(BF16)
+            scales.append(scale)
+            u.append((unit * gain1[n : n + 1] + bias1[n : n + 1]).astype(BF16))
+        xl, xsm = analyse(tl[...], ts[...], side(u))
+        yl, ys = [], []
+        for j, (a, b) in enumerate(zip(lanes(xl), lanes(xsm))):
+            spec[n, j, : 2 * NL] = a.astype(BF16)
+            spec[n, j, 2 * NL :] = b.astype(BF16)
+            lr, li = a[:NL], a[NL:]
+            sr, si = b[: PER * NS], b[PER * NS :]
+            gr, gi = filt_l[n, 0], filt_l[n, 1]
+            yl.append(jnp.concatenate([lr * gr - li * gi, lr * gi + li * gr], axis=0).astype(BF16))
+            gr, gi = thrice(filt_s[n, 0]), thrice(filt_s[n, 1])
+            ys.append(jnp.concatenate([sr * gr - si * gi, sr * gi + si * gr], axis=0).astype(BF16))
         v = []
-        for j in range(pair):
-            xs[n, j] = x[j]
-            u, _ = normal(x[j])
-            u = (u * gain1[n : n + 1] + bias1[n : n + 1]).astype(BF16)
-            xl, xsm = analyse(tl[...], ts[...], u)
-            spec[n, j, : 2 * NL] = xl
-            spec[n, j, 2 * NL :] = xsm
-            lr, li = xl[:NL], xl[NL:]
-            sr, si = xsm[: PER * NS], xsm[PER * NS :]
-            gr, gi = filt_l[n, 0], filt_l[n, 1]
-            yl = jnp.concatenate([lr * gr - li * gi, lr * gi + li * gr], axis=0).astype(BF16)
-            gr, gi = thrice(filt_s[n, 0]), thrice(filt_s[n, 1])
-            ys = jnp.concatenate([sr * gr - si * gi, sr * gi + si * gr], axis=0).astype(BF16)
-            z = synthesise(tlb[...], tsb[...], yl, ys)
-            zs[n, j] = z
-            q, _ = normal(z)
-            q = (q * gain2[n : n + 1] + bias2[n : n + 1]).astype(BF16)
-            vs[n, j] = q
-            v.append(q)
+        for j, z in enumerate(lanes(synthesise(tlb[...], tsb[...], side(yl), side(ys)))):
+            unit, scale = normal(z)
+            zs[n, j] = unit.astype(BF16)
+            both_scales[n, j] = side([scales[j], scale])
+            unit = (unit * gain2[n : n + 1] + bias2[n : n + 1]).astype(BF16)
+            vs[n, j] = unit
+            v.append(unit)
         v = jnp.concatenate(v, axis=0)
         total = jnp.concatenate(x, axis=0) + b2[n : n + 1]
         for c in range(0, FF, CH):
@@ -251,29 +274,32 @@
             @pl.loop(0, groups)
             def _(g):
                 for m in range(1, row_count):
-                    remote(which, m, g).wait_send()
-
-
-def forward(mesh, groups, pair, packed_in, packed_cot, counts, bounds, small):
+                    for copy in remote(which, m, g):
+                        copy.wait_send()
+
+
+def forward(mesh, groups, pair, crops, counts, bounds, small):
     rows = mesh.shape["rows"]
-    sizes = [(T, D, F32), (T, D, F32), (2 * NL + 2 * PER * NS, D, F32), (T, D, BF16), (T, FF, BF16), (T, FF, BF16)]
+    sizes = [(T, D, BF16), (T, D, BF16), (T, 2, F32), (2 * NL + 2 * PER * NS, D, BF16), (T, D, BF16), (T, FF, BF16), (T, FF, BF16)]
     extra = [((groups, T, D), BF16), ((rows * BAND, T), BF16), ((LAYERS, 2, NL, D), F32), ((LAYERS, 2, NS, D), F32), ((NS, NL), F32)]
     hbm = pl.BlockSpec(memory_space=pl.ANY)
     return pl.pallas_call(
         partial(forward_kernel, rows, groups, pair),
         grid=(groups // pair,),
-        in_specs=[hbm, hbm, scalars(), scalars()] + [whole(a.shape) for a in small],
+        in_specs=[hbm] * 4 + [scalars(), scalars()] + [whole(a.shape) for a in small],
         out_specs=[pl.BlockSpec((rows, pair, BAND, D), lambda i: (0, i, 0, 0))]
         + [pl.BlockSpec((LAYERS, pair, a, b), lambda i: (0, i, 0, 0)) for a, b, _ in sizes]
         + [whole(a) for a, _ in extra],
         out_shape=[jax.ShapeDtypeStruct((rows, groups, BAND, D), BF16)]
         + [jax.ShapeDtypeStruct((LAYERS, groups, a, b), t) for a, b, t in sizes]
         + [jax.ShapeDtypeStruct(a, t) for a, t in extra],
-        scratch_shapes=[pltpu.VMEM((T, rows * BAND), BF16), pltpu.VMEM((2, rows, groups, BAND, D), BF16), pltpu.SemaphoreType.DMA((2, groups)),
-                        pltpu.SemaphoreType.DMA((2, rows - 1, groups)), pltpu.SemaphoreType.DMA((2, rows - 1, groups))],
+        scratch_shapes=[pltpu.VMEM((T, rows * BAND), BF16), pltpu.VMEM((rows * BAND, D), F32),
+                        pltpu.VMEM((2, rows, groups, WL, BL, D), BF16), pltpu.VMEM((2, rows, groups, PER, WS, BS, D), BF16),
+                        pltpu.SemaphoreType.DMA((2, 2, groups)), pltpu.SemaphoreType.DMA((2, 2, rows - 1, groups)),
+                        pltpu.SemaphoreType.DMA((2, 2, rows - 1, groups))],
         compiler_params=pltpu.CompilerParams(collective_id=1, has_side_effects=True, vmem_limit_bytes=VMEM_LIMIT),
         name="forward",
-    )(packed_in, packed_cot, counts, bounds, *small)
+    )(*crops, counts, bounds, *small)
 
 
 SPREAD = True
@@ -395,7 +421,7 @@
 
 
 def backward_kernel(row_count, batch_count, groups, pair, place, filt_l, filt_s, gain1, gain2, w1, w2, tl, ts, tlb, tsb,
-                    mix, fold, outs, do_in, xs, zs, spec, vs, gs, ps,
+                    mix, fold, outs, do_in, xs, zs, both_scales, spec, vs, gs, ps,
                     out_land, grad_land, weights_out, small_out,
                     dx, dv, do, dot_, vt, dh, gslots, dvec, dhid, dfl, dfs, out_sem, grad_sem, own_sem, *sums):
     i = pl.program_id(0)
@@ -512,43 +538,52 @@
 
     @pl.when((i < compute_steps) & (q >= chunks))
     def _():
+        side = lambda parts: jnp.concatenate(parts, axis=1)
+        lanes = lambda a: [a[:, j * D : (j + 1) * D] for j in range(pair)]
+        row_sum = lambda a: jnp.sum(a, axis=0, keepdims=True)
+        first = (q - chunks) * pair
+        dz = []
         for j in range(pair):
-            if j:
-                advance(2 * j - 1, second_steps)
-            g = (q - chunks) * pair + j
-            dvg = dv[g]
-            u, scale = normal(zs[0, j])
-            row_sum = lambda a: jnp.sum(a, axis=0, keepdims=True)
-            dvec[layer, 2:3] += row_sum(dvg * u)
+            dvg = dv[first + j]
+            unit = zs[0, j].astype(F32)
+            dvec[layer, 2:3] += row_sum(dvg * unit)
             dvec[layer, 3:4] += row_sum(dvg)
-            dz = normal_back(dvg, gain2[pl.ds(layer, 1)], u, scale).astype(BF16)
-            yl, ysm = analyse(tl[...], ts[...], dz)
-            lr, li = yl[:NL], yl[NL:]
-            sr, si = ysm[: PER * NS], ysm[PER * NS :]
-            xr, xi = spec[0, j, :NL], spec[0, j, NL : 2 * NL]
+            dz.append(normal_back(dvg, gain2[pl.ds(layer, 1)], unit, both_scales[0, j, :, 1:2]).astype(BF16))
+        advance(0, second_steps)
+        yl, ysm = analyse(tl[...], ts[...], side(dz))
+        dl, ds = [], []
+        for j, (a, b) in enumerate(zip(lanes(yl), lanes(ysm))):
+            lr, li = a[:NL], a[NL:]
+            sr, si = b[: PER * NS], b[PER * NS :]
+            xr, xi = spec[0, j, :NL].astype(F32), spec[0, j, NL : 2 * NL].astype(F32)
             dfl[layer, :NL] += lr * xr + li * xi
             dfl[layer, NL:] += li * xr - lr * xi
-            advance(2 * j, second_steps)
             gr, gi = filt_l[0, 0], filt_l[0, 1]
-            dl = jnp.concatenate([lr * gr + li * gi, li * gr - lr * gi], axis=0).astype(BF16)
-            xr, xi = spec[0, j, 2 * NL : 2 * NL + PER * NS], spec[0, j, 2 * NL + PER * NS :]
+            dl.append(jnp.concatenate([lr * gr + li * gi, li * gr - lr * gi], axis=0).astype(BF16))
+            small_spec = spec[0, j, 2 * NL :].astype(F32)
+            xr, xi = small_spec[: PER * NS], small_spec[PER * NS :]
             once = lambda a: a[:NS] + a[NS : 2 * NS] + a[2 * NS :]
             dfs[layer, :NS] += once(sr * xr + si * xi)
             dfs[layer, NS:] += once(si * xr - sr * xi)
             gr, gi = thrice(filt_s[0, 0]), thrice(filt_s[0, 1])
-            ds = jnp.concatenate([sr * gr + si * gi, si * gr - sr * gi], axis=0).astype(BF16)
-            du = synthesise(tlb[...], tsb[...], dl, ds)
-            u, scale = normal(xs[0, j])
-            dvec[layer, 0:1] += row_sum(du * u)
+            ds.append(jnp.concatenate([sr * gr + si * gi, si * gr - sr * gi], axis=0).astype(BF16))
+        advance(1, second_steps)
+        grads = []
+        for j, du in enumerate(lanes(synthesise(tlb[...], tsb[...], side(dl), side(ds)))):
+            unit = xs[0, j].astype(F32)
+            dvec[layer, 0:1] += row_sum(du * unit)
             dvec[layer, 1:2] += row_sum(du)
-            grad = dx[g] + normal_back(du, gain1[pl.ds(layer, 1)], u, scale)
-            dx[g] = grad
-
-            @pl.when(layer == 0)
-            def _():
-                spread = dot(place[...], grad.astype(BF16)).astype(BF16)
+            grad = dx[first + j] + normal_back(du, gain1[pl.ds(layer, 1)], unit, both_scales[0, j, :, 0:1])
+            dx[first + j] = grad
+            grads.append(grad.astype(BF16))
+        advance(2, second_steps)
+
+        @pl.when(layer == 0)
+        def _():
+            spread = dot(place[...], side(grads)).astype(BF16)
+            for j in range(pair):
                 for m in range(row_count):
-                    gslots[m, g] = spread[m * BAND : (m + 1) * BAND]
+                    gslots[m, first + j] = spread[m * BAND : (m + 1) * BAND, j * D : (j + 1) * D]
 
     @pl.when(i == compute_steps - 1)
     def _():
@@ -597,7 +632,7 @@
     per_layer = lambda a: pl.BlockSpec((1,) + a.shape[1:], lambda i: (layer(i),) + (0,) * (a.ndim - 1))
     by_pair = lambda a: pl.BlockSpec((1, pair) + a.shape[2:], lambda i: (layer(i), place_of(i), 0, 0))
     by_chunk = lambda a: pl.BlockSpec((1, groups, T, CB), lambda i: (layer(i), 0, 0, chunk(i)))
-    xs, zs, spec, vs, gs, ps = saved
+    xs, zs, scales, spec, vs, gs, ps = saved
     hbm = pl.BlockSpec(memory_space=pl.ANY)
     width = columns(rows, batch)
     part_rows, small_rows = padded(rows, batch, 2 * D * (CB // width)), padded(rows, batch, SMALL)
@@ -608,7 +643,7 @@
         in_specs=[whole(place.shape), per_layer(filt_l), per_layer(filt_s), whole(gain1.shape), whole(gain2.shape)]
         + [pl.BlockSpec((1, D, CB), lambda i: (layer(i), 0, chunk(i))), pl.BlockSpec((1, CB, D), lambda i: (layer(i), chunk(i), 0))]
         + [whole(a.shape) for a in (*tabs, mix, fold)] + [hbm, whole(do.shape)]
-        + [by_pair(xs), by_pair(zs), by_pair(spec), per_layer(vs), by_chunk(gs), by_chunk(ps)],
+        + [by_pair(xs), by_pair(zs), by_pair(scales), by_pair(spec), per_layer(vs), by_chunk(gs), by_chunk(ps)],
         out_specs=[hbm] * 4,
         out_shape=[jax.ShapeDtypeStruct((rows, groups, BAND, D), BF16)] * 2
         + [jax.ShapeDtypeStruct((LAYERS * chunks * part_rows, width), BF16), jax.ShapeDtypeStruct((small_rows, D), BF16)],
@@ -621,73 +656,103 @@
         + sum_scratch(rows, batch, LAYERS * chunks, part_rows, width) + sum_scratch(rows, batch, 1, small_rows, D),
         compiler_params=pltpu.CompilerParams(collective_id=2, has_side_effects=True, vmem_limit_bytes=VMEM_LIMIT),
         name="backward",
-    )(place, filt_l, filt_s, gain1, gain2, w1, w2, *tabs, mix, fold, outs, do, xs, zs, spec, vs, gs, ps)
-
-
-def unpack_kernel(order, outs, grads, weights, small, large_out, small_crops, large_grad, small_grad, dw1, dw2,
-                  dfilter, dvec, dhid):
-    i = pl.program_id(0)
-    for given, large, little in ((outs, large_out, small_crops), (grads, large_grad, small_grad)):
-        for g in range(given.shape[1]):
-            block = given[0, g].astype(F32)
-            for s in range(WL):
-                large[g, 0, s] = block[s * BL : (s + 1) * BL]
-            for p in range(PER):
-                for s in range(WS):
-                    at = BL * WL + (p * WS + s) * BS
-                    little[g * PER + p, 0, s] = block[at : at + BS]
-    width = weights.shape[1]
-    parts = CB // width
-    for c in range(parts):
-        cols = slice(c * width, (c + 1) * width)
-        dw1[0, :, cols] = weights[c * D : (c + 1) * D, :].astype(F32)
-        dw2[0, cols, :] = weights[(parts + c) * D : (parts + c + 1) * D, :].astype(F32).T
-
-    @pl.when(i == 0)
-    def _():
-        at = LAYERS * 2 * NL
-        for n in range(LAYERS):
-            for c in range(2):
-                dfilter[n, c] = small[(n * 2 + c) * NL : (n * 2 + c + 1) * NL].astype(F32)
-        rest = small[at : at + 32].astype(F32)
-        for n in range(LAYERS):
-            for k in range(5):
-                dvec[k, n : n + 1] = rest[n * 5 + k : n * 5 + k + 1]
-            for c in range(FF // D):
-                r = LAYERS * 5 + n * (FF // D) + c
-                dhid[n : n + 1, c * D : (c + 1) * D] = rest[r : r + 1]
-
-
-def unpack(mesh, groups, outs, grads, weights, small):
+    )(place, filt_l, filt_s, gain1, gain2, w1, w2, *tabs, mix, fold, outs, do, xs, zs, scales, spec, vs, gs, ps)
+
+
+def unpack_kernel(groups, order, outs, grads, weights, small, large_out, small_crops, large_grad, small_grad, dw1, dw2, dfilter, dhid,
+                  *rest):
+    dvec, rest = rest[:5], rest[5:]
+    given, weight, large, little, one, two, in_sem, weight_sem, out_sem, done_sem = rest
+    rows = outs.shape[0]
+    parts, chunks, width = weight.shape[0], FF // CB, weight.shape[2]
+    halves = CB // width
+
+    def read(dev, kind):
+        return pltpu.make_async_copy((outs, grads)[kind].at[order[dev]], given.at[kind, dev], in_sem.at[kind, dev])
+
+    def read_weight(part):
+        return pltpu.make_async_copy(weights.at[part], weight.at[part], weight_sem.at[part])
+
+    def write(dev, kind):
+        to_large, to_little = ((large_out, small_crops), (large_grad, small_grad))[kind]
+        return (pltpu.make_async_copy(large.at[kind, dev], to_large.at[pl.ds(dev * groups, groups)], out_sem.at[kind, 0, dev]),
+                pltpu.make_async_copy(little.at[kind, dev], to_little.at[pl.ds(dev * groups * PER, groups * PER)], out_sem.at[kind, 1, dev]))
+
+    def write_weight(part):
+        layer, at = LAYERS - 1 - part // chunks, part % chunks * CB
+        return (pltpu.make_async_copy(one.at[part], dw1.at[layer, :, pl.ds(at, CB)], done_sem.at[0, part]),
+                pltpu.make_async_copy(two.at[part], dw2.at[layer, pl.ds(at, CB)], done_sem.at[1, part]))
+
+    for part in range(parts):
+        read_weight(part).start()
+    for dev in range(rows):
+        for kind in range(2):
+            read(dev, kind).start()
+    for part in range(parts):
+        read_weight(part).wait()
+        for c in range(halves):
+            cols = slice(c * width, (c + 1) * width)
+            one[part, :, cols] = weight[part, c * D : (c + 1) * D].astype(F32)
+            two[part, cols] = weight[part, (halves + c) * D : (halves + c + 1) * D].astype(F32).T
+        for copy in write_weight(part):
+            copy.start()
+    for dev in range(rows):
+        for kind in range(2):
+            read(dev, kind).wait()
+
+            @pl.loop(0, groups)
+            def _(g):
+                block = given[kind, dev, g].astype(F32)
+                for w in range(WL):
+                    large[kind, dev, g, 0, w] = block[w * BL : (w + 1) * BL]
+                for p in range(PER):
+                    for w in range(WS):
+                        at = BL * WL + (p * WS + w) * BS
+                        little[kind, dev, g * PER + p, 0, w] = block[at : at + BS]
+
+            for copy in write(dev, kind):
+                copy.start()
+    at = LAYERS * 2 * NL
+    for n in range(LAYERS):
+        for c in range(2):
+            dfilter[n, c] = small[(n * 2 + c) * NL : (n * 2 + c + 1) * NL].astype(F32)
+    others = small[at : at + 32].astype(F32)
+    for n in range(LAYERS):
+        for k in range(5):
+            dvec[k][n : n + 1] = others[n * 5 + k : n * 5 + k + 1]
+        for c in range(FF // D):
+            r = LAYERS * 5 + n * (FF // D) + c
+            dhid[n : n + 1, c * D : (c + 1) * D] = others[r : r + 1]
+    for part in range(parts):
+        for copy in write_weight(part):
+            copy.wait()
+    for dev in range(rows):
+        for kind in range(2):
+            for copy in write(dev, kind):
+                copy.wait()
+
+
+def unpack(mesh, groups, pair, outs, grads, weights, small):
     rows = mesh.shape["rows"]
     me = lax.axis_index("rows")
     crops = rows * groups
-    chunks = FF // CB
-    parts = LAYERS * chunks
-    steps = max(rows, parts)
-    order = (jnp.arange(rows, dtype=jnp.int32) - me) % rows
-    dev = lambda i: jnp.minimum(i, rows - 1)
-    part = lambda i: jnp.minimum(i, parts - 1)
-    part_rows = weights.shape[0] // parts
-    given = pl.BlockSpec((1, groups, BAND, D), lambda i, order: (order[dev(i)], 0, 0, 0))
-    large = pl.BlockSpec((groups, 1, WL, BL, D), lambda i, order: (dev(i), 0, 0, 0, 0))
-    little = pl.BlockSpec((groups * PER, 1, WS, BS, D), lambda i, order: (dev(i), 0, 0, 0, 0))
-    every = lambda shape: pl.BlockSpec(shape, lambda i, order: (0,) * len(shape))
-    large_shape = jax.ShapeDtypeStruct((crops, 1, WL, BL, D), F32)
-    little_shape = jax.ShapeDtypeStruct((crops * PER, 1, WS, BS, D), F32)
-    shapes = [(LAYERS, 2, NL, D), (5, LAYERS, D), (LAYERS, FF)]
+    width = weights.shape[1]
+    halves = CB // width
+    parts = LAYERS * (FF // CB)
+    weights = weights.reshape(parts, -1, width)[:, : 2 * D * halves]
+    order = lax.rem(jnp.arange(rows, dtype=jnp.int32) + (rows - me), rows)
+    large_shape, little_shape = (crops, 1, WL, BL, D), (crops * PER, 1, WS, BS, D)
+    shapes = [(LAYERS, 2, NL, D), (LAYERS, FF)] + [(LAYERS, D)] * 5
+    hbm, vmem, dma = pl.BlockSpec(memory_space=pl.ANY), pl.BlockSpec(memory_space=pltpu.VMEM), pltpu.SemaphoreType.DMA
     return pl.pallas_call(
-        unpack_kernel,
-        grid_spec=pltpu.PrefetchScalarGridSpec(
-            num_scalar_prefetch=1, grid=(steps,),
-            in_specs=[given, given, pl.BlockSpec((part_rows, weights.shape[1]), lambda i, order: (part(i), 0)), every(small.shape)],
-            out_specs=[large, little, large, little,
-                       pl.BlockSpec((1, D, CB), lambda i, order: (LAYERS - 1 - part(i) // chunks, 0, part(i) % chunks)),
-                       pl.BlockSpec((1, CB, D), lambda i, order: (LAYERS - 1 - part(i) // chunks, part(i) % chunks, 0))]
-            + [every(s) for s in shapes]),
-        out_shape=[large_shape, little_shape, large_shape, little_shape,
-                   jax.ShapeDtypeStruct((LAYERS, D, FF), F32), jax.ShapeDtypeStruct((LAYERS, FF, D), F32)]
-        + [jax.ShapeDtypeStruct(s, F32) for s in shapes],
+        partial(unpack_kernel, groups),
+        in_specs=[scalars()] + [hbm] * 3 + [vmem],
+        out_specs=[hbm] * 6 + [vmem] * len(shapes),
+        out_shape=[jax.ShapeDtypeStruct(s, F32) for s in [large_shape, little_shape] * 2 + [(LAYERS, D, FF), (LAYERS, FF, D)] + shapes],
+        scratch_shapes=[pltpu.VMEM((2, rows, groups, BAND, D), BF16), pltpu.VMEM(weights.shape, BF16),
+                        pltpu.VMEM((2, rows, groups, 1, WL, BL, D), F32), pltpu.VMEM((2, rows, groups * PER, 1, WS, BS, D), F32),
+                        pltpu.VMEM((parts, D, CB), F32), pltpu.VMEM((parts, CB, D), F32),
+                        dma((2, rows)), dma((parts,)), dma((2, 2, rows)), dma((2, parts))],
         compiler_params=pltpu.CompilerParams(vmem_limit_bytes=VMEM_LIMIT),
         name="unpack",
     )(order, outs, grads, weights, small)
@@ -725,21 +790,17 @@
     tabs = tables()
     filters = filters.reshape(LAYERS, 2, NL, D)
 
-    def pack(large, small):
-        return jnp.concatenate([large.transpose(0, 1, 3, 2, 4).reshape(crops, BL * WL, D),
-                                small.transpose(0, 1, 3, 2, 4).reshape(crops, PER * BS * WS, D),
-                                jnp.zeros((crops, BAND - BL * WL - PER * BS * WS, D), large.dtype)], axis=1)
-
+    arrays = [a.transpose(0, 1, 3, 2, 4) for a in (large_in, small_in, large_cot, small_cot)]
     need, slot = wanted_rows()
     extras = (jnp.asarray(need), jnp.asarray(slot), row_interp, col_interp, *interp_tables())
-    outs, *saved, do, place, filt_l, filt_s, mix = forward(mesh, groups, pair, pack(large_in, small_in), pack(large_cot, small_cot), crop_counts, band_bounds,
+    outs, *saved, do, place, filt_l, filt_s, mix = forward(mesh, groups, pair, arrays, crop_counts, band_bounds,
                                (filters, norm1_gain, norm1_bias, norm2_gain, norm2_bias, fc1_weight, fc1_bias, fc2_weight, fc2_bias,
                                 *tabs, *extras))
     outs, grads, weights, small = backward(
         mesh, groups, pair, (place, filt_l, filt_s, norm1_gain, norm2_gain, fc1_weight, fc2_weight), tabs,
         mix, extras[-1], outs, do, saved)
-    large_out, small_out, large_grad, small_grad, dw1, dw2, dfilter, dvec, dhid = unpack(
-        mesh, groups, outs, grads, weights, small)
+    large_out, small_out, large_grad, small_grad, dw1, dw2, dfilter, dhid, *dvec = unpack(
+        mesh, groups, pair, outs, grads, weights, small)
     large_out, small_out, large_grad, small_grad = (
         a.transpose(0, 1, 3, 2, 4) for a in (large_out, small_out, large_grad, small_grad))
     return (large_out, small_out, large_grad, small_grad, dvec[0], dvec[1], dfilter.reshape(LAYERS, 2, HL, FL, D), dvec[2], dvec[3],

time: 173 us -> 158 us (0.913)
  local copies, waits for them, and re-layouts: 7.58 us -> 0 us
  Pallas kernels: 160 us -> 156 us
  other arithmetic: 3.51 us -> 0.58 us
    reshape x4 -> x0, local copies, waits for them, and re-layouts: 6.2 us -> none  [the longest x2 4.17 us: pack(): small.transpose(0, 1, 3, 2, 4).reshape(crops, PER * BS * WS, D)]
    concatenate x1 -> x0, other arithmetic: 2.99 us -> none  [pack(): jnp.concatenate([large.transpose(0, 1, 3, 2, 4).reshape(crops, BL * WL, D...]
    pallas_call x1, Pallas kernels: 96.9 us -> 94.6 us  [backward(): pl.pallas_call(partial(backward_kernel, rows, batch, groups, pair), grid=...]
where the time goes in v3:
time: 158 us
  Pallas kernels  156 us (99%)
    pallas_call x1, Pallas kernels, backward(): pl.pallas_call(partial(backward_kernel, rows, batch, groups, pair), grid=...  94.6 us
    pallas_call x1, Pallas kernels, forward(): pl.pallas_call(partial(forward_kernel, rows, groups, pair), grid=(groups...  50.4 us
    pallas_call x1, Pallas kernels, unpack(): pl.pallas_call(partial(unpack_kernel, groups), in_specs=[scalars()] + [hb...  11.1 us

profile of v3, /device:TPU:0, one launch (start us, length us, event | category | flops | bytes accessed | tf_op | source)
XLA Modules:
  0.0 157.6 jit_solution(1485212577473608809)
XLA Ops:
  0.6 50.4 %forward.1 = (bf16[4,6,96,384]{3,2,1,0:T(8,128)(2,1)}, bf16[2,6,304,384]{3,2,1,0:T(8,128)(2,1)}, bf16[2,6,304,384]{3,2,1,0:T(8,128)(2,1)}, f32[2,6,304,2]{3,2,1,...) custom-call(bf16[24,1,14,4,384]{4,3,2,1,0:T(4,128)(2,1)} %bitcast.12, ...), custom_call_target="tpu_custom_call" | custom-call | tf_op jit(solution)/shard_map/forward/pallas_call | solution.py:286
  51.1 94.6 %backward.1 = (bf16[4,6,96,384]{3,2,1,0:T(8,128)(2,1)}, bf16[4,6,96,384]{3,2,1,0:T(8,128)(2,1)}, bf16[9216,256]{1,0:T(8,128)(2,1)}, bf16[512,384]{1,0:T(8,128)(2,1)}) custom-call(bf16[384,304]{1,0:T(8,128)(2,1)} %get-tuple-element.43.place, f32[2,2,112,384]{3,2,1,0:T(8,128)} %get-tuple-element.44.filt_l, f32[2,2,24,384]{3,2,1,0:T(8,128)} %get-tuple-element.45.filt_s, ...), custom_call_target="tpu_custom_call" | custom-call | tf_op jit(solution)/shard_map/backward/pallas_call | solution.py:640
  145.7 0.6 compare_select_fusion.order
  146.3 11.1 %unpack.1 = (f32[24,1,14,4,384]{4,3,2,1,0:T(4,128)}, f32[72,1,6,2,384]{4,3,2,1,0:T(2,128)}, f32[24,1,14,4,384]{4,3,2,1,0:T(4,128)}, f32[72,1,6,2,384]{4,3,2,1,0:...) custom-call(s32[4]{0:T(128)} %compare_select_fusion.order, ...), custom_call_target="tpu_custom_call" | custom-call | tf_op jit(solution)/shard_map/unpack/pallas_call | solution.py:747

commit v4 on v3

--- a/solution.py
+++ b/solution.py
@@ -30,26 +30,26 @@
     (1, 9): [(1, 0)],
     (2, 0): [(-3, 3)],
     (2, 2): [(1, 1)],
-    (2, 9): [(0, 2), (2, 0)],
-    (3, 0): [(-3, 4)],
+    (2, 9): [(2, 0), (-3, 4)],
+    (3, 0): [(0, 2)],
     (3, 2): [(2, 1)],
     (4, 0): [(-3, 5)],
-    (4, 1): [(1, 2)],
-    (5, 1): [(0, 3)],
-    (5, 2): [(2, 2)],
-    (6, 9): [(1, 3), (3, 0)],
-    (7, 1): [(0, 4)],
-    (7, 2): [(3, 1)],
-    (7, 9): [(4, 0), (2, 3)],
+    (4, 2): [(1, 2)],
+    (5, 9): [(2, 2)],
+    (6, 0): [(0, 3)],
+    (6, 9): [(3, 0)],
+    (7, 0): [(1, 3)],
+    (7, 1): [(3, 1)],
+    (7, 9): [(2, 3), (4, 0)],
     (8, 2): [(4, 1)],
-    (8, 9): [(1, 4), (0, 5), (5, 0)],
-    (9, 1): [(3, 2)],
-    (9, 2): [(0, 6)],
-    (9, 9): [(5, 1), (2, 4), (-2, 0)],
+    (8, 9): [(0, 4), (3, 2), (5, 0)],
+    (9, 2): [(5, 1), (1, 4)],
+    (9, 9): [(-2, 0)],
     (10, 1): [(4, 2)],
+    (10, 9): [(2, 4)],
     (11, 0): [(-2, 1)],
-    (11, 1): [(1, 5)],
-    (11, 9): [(3, 3), (-1, 0), (1, 6), (5, 2), (-1, 1), (4, 3), (2, 5), (-1, 2), (2, 6), (3, 4), (-2, 2), (5, 3), (3, 5), (-2, 3), (4, 4), (3, 6), (-1, 3), (5, 4), (-2, 4), (4, 5), (-1, 4), (-2, 5), (4, 6), (5, 5), (-1, 5), (5, 6), (-1, 6)],
+    (11, 1): [(0, 5)],
+    (11, 9): [(-1, 0), (0, 6), (-2, 2), (3, 3), (5, 2), (-1, 1), (4, 3), (1, 5), (1, 6), (2, 5), (-1, 2), (-2, 3), (2, 6), (3, 4), (5, 3), (4, 4), (-2, 4), (3, 5), (3, 6), (-1, 3), (5, 4), (-2, 5), (4, 5), (4, 6), (-1, 4), (5, 5), (-1, 5), (5, 6), (-1, 6)],
 }
 MESH = pl.DeviceIdType.MESH
 VMEM_LIMIT = 60 * 2**20
@@ -142,9 +142,9 @@
 
 
 def forward_kernel(row_count, groups, pair, large_in, small_in, large_cot, small_cot, counts, bounds, filters, gain1, bias1, gain2, bias2,
-                   w1, b1, w2, b2, tl, ts, tlb, tsb, need, slot, row_interp, col_interp, row_s, row_l, col_s, col_l, fold,
-                   outs, xs, zs, both_scales, spec, vs, gs, ps, do, place, filt_l, filt_s, mix,
-                   pick, lined, large_slots, small_slots, own_sem, send_sem, recv_sem):
+                   w1_in, b1, w2_in, b2, tl, ts, tlb, tsb, need, slot, row_interp, col_interp, row_s, row_l, col_s, col_l, fold,
+                   outs, xs, zs, both_scales, spec, vs, gs_out, ps_out, do, place, filt_l, filt_s, mix,
+                   w1, w2, gs, ps, weight_sem, save_sem, pick, lined, large_slots, small_slots, own_sem, send_sem, recv_sem):
     step = pl.program_id(0)
     batch, row = lax.axis_index("batch"), lax.axis_index("rows")
     last = groups // pair - 1
@@ -164,6 +164,15 @@
     def mine(which, g):
         return [pltpu.make_async_copy(source, target, own_sem.at[which, k, g])
                 for k, (source, target) in enumerate(ends(which, 0, g, row))]
+
+    def weights(n):
+        return [pltpu.make_async_copy(w1_in.at[n], w1.at[n], weight_sem.at[0, n]),
+                pltpu.make_async_copy(w2_in.at[n], w2.at[n], weight_sem.at[1, n])]
+
+    def keep(n, c, at):
+        cols = pl.ds(c, CH)
+        return [pltpu.make_async_copy(ref.at[n, :, :, cols], out.at[n, pl.ds(at * pair, pair), :, cols], save_sem.at[k, n, c // CH])
+                for k, (ref, out) in enumerate(((gs, gs_out), (ps, ps_out)))]
 
     @pl.when(step == 0)
     def _():
@@ -182,6 +191,9 @@
                 for m in range(1, row_count):
                     for copy in remote(which, m, g):
                         copy.start()
+        for n in range(LAYERS):
+            for copy in weights(n):
+                copy.start()
         lined[...] = jnp.zeros_like(lined)
         for m in range(row_count):
             band = lax.rem(row + (row_count - m), row_count)
@@ -251,6 +263,17 @@
             v.append(unit)
         v = jnp.concatenate(v, axis=0)
         total = jnp.concatenate(x, axis=0) + b2[n : n + 1]
+        @pl.when(step == 0)
+        def _():
+            for copy in weights(n):
+                copy.wait()
+
+        @pl.when(step > 0)
+        def _():
+            for c in range(0, FF, CH):
+                for copy in keep(n, c, step - 1):
+                    copy.wait()
+
         for c in range(0, FF, CH):
             h = dot(v, w1[n, :, c : c + CH]) + b1[n : n + 1, c : c + CH]
             g, slope = gelu_both(h)
@@ -259,6 +282,8 @@
             for j in range(pair):
                 gs[n, j, :, c : c + CH] = g[j * T : (j + 1) * T]
                 ps[n, j, :, c : c + CH] = slope[j * T : (j + 1) * T]
+            for copy in keep(n, c, step):
+                copy.start()
             total = total + dot(g, w2[n, c : c + CH, :])
         x = [total[j * T : (j + 1) * T] for j in range(pair)]
     for j in range(pair):
@@ -276,6 +301,10 @@
                 for m in range(1, row_count):
                     for copy in remote(which, m, g):
                         copy.wait_send()
+        for n in range(LAYERS):
+            for c in range(0, FF, CH):
+                for copy in keep(n, c, last):
+                    copy.wait()
 
 
 def forward(mesh, groups, pair, crops, counts, bounds, small):
@@ -286,14 +315,17 @@
     return pl.pallas_call(
         partial(forward_kernel, rows, groups, pair),
         grid=(groups // pair,),
-        in_specs=[hbm] * 4 + [scalars(), scalars()] + [whole(a.shape) for a in small],
+        in_specs=[hbm] * 4 + [scalars(), scalars()] + [hbm if a.shape[1:] in ((D, FF), (FF, D)) else whole(a.shape) for a in small],
         out_specs=[pl.BlockSpec((rows, pair, BAND, D), lambda i: (0, i, 0, 0))]
-        + [pl.BlockSpec((LAYERS, pair, a, b), lambda i: (0, i, 0, 0)) for a, b, _ in sizes]
+        + [pl.BlockSpec((LAYERS, pair, a, b), lambda i: (0, i, 0, 0)) if b != FF else hbm for a, b, _ in sizes]
         + [whole(a) for a, _ in extra],
         out_shape=[jax.ShapeDtypeStruct((rows, groups, BAND, D), BF16)]
         + [jax.ShapeDtypeStruct((LAYERS, groups, a, b), t) for a, b, t in sizes]
         + [jax.ShapeDtypeStruct(a, t) for a, t in extra],
-        scratch_shapes=[pltpu.VMEM((T, rows * BAND), BF16), pltpu.VMEM((rows * BAND, D), F32),
+        scratch_shapes=[pltpu.VMEM((LAYERS, D, FF), BF16), pltpu.VMEM((LAYERS, FF, D), BF16)]
+        + [pltpu.VMEM((LAYERS, pair, T, FF), BF16)] * 2
+        + [pltpu.SemaphoreType.DMA((2, LAYERS)), pltpu.SemaphoreType.DMA((2, LAYERS, FF // CH)),
+                        pltpu.VMEM((T, rows * BAND), BF16), pltpu.VMEM((rows * BAND, D), F32),
                         pltpu.VMEM((2, rows, groups, WL, BL, D), BF16), pltpu.VMEM((2, rows, groups, PER, WS, BS, D), BF16),
                         pltpu.SemaphoreType.DMA((2, 2, groups)), pltpu.SemaphoreType.DMA((2, 2, rows - 1, groups)),
                         pltpu.SemaphoreType.DMA((2, 2, rows - 1, groups))],

time: 158 us -> 152 us (0.962)
  Pallas kernels: 156 us -> 150 us
    pallas_call x1, Pallas kernels: 50.4 us -> 46.6 us  [forward(): pl.pallas_call(partial(forward_kernel, rows, groups, pair), grid=(groups...]
    pallas_call x1, Pallas kernels: 94.6 us -> 92.8 us  [backward(): pl.pallas_call(partial(backward_kernel, rows, batch, groups, pair), grid=...]
where the time goes in v4:
time: 152 us
  Pallas kernels  150 us (99%)
    pallas_call x1, Pallas kernels, backward(): pl.pallas_call(partial(backward_kernel, rows, batch, groups, pair), grid=...  92.8 us
    pallas_call x1, Pallas kernels, forward(): pl.pallas_call(partial(forward_kernel, rows, groups, pair), grid=(groups...  46.6 us
    pallas_call x1, Pallas kernels, unpack(): pl.pallas_call(partial(unpack_kernel, groups), in_specs=[scalars()] + [hb...  11.1 us

profile of v4, /device:TPU:0, one launch (start us, length us, event | category | flops | bytes accessed | tf_op | source)
XLA Modules:
  0.0 151.9 jit_solution(10811837492270125306)
XLA Ops:
  0.6 46.6 %forward.1 = (bf16[4,6,96,384]{3,2,1,0:T(8,128)(2,1)}, bf16[2,6,304,384]{3,2,1,0:T(8,128)(2,1)}, bf16[2,6,304,384]{3,2,1,0:T(8,128)(2,1)}, f32[2,6,304,2]{3,2,1,...) custom-call(bf16[24,1,14,4,384]{4,3,2,1,0:T(4,128)(2,1)} %bitcast.12, ...), custom_call_target="tpu_custom_call" | custom-call | tf_op jit(solution)/shard_map/forward/pallas_call | solution.py:315
  47.2 92.8 %backward.1 = (bf16[4,6,96,384]{3,2,1,0:T(8,128)(2,1)}, bf16[4,6,96,384]{3,2,1,0:T(8,128)(2,1)}, bf16[9216,256]{1,0:T(8,128)(2,1)}, bf16[512,384]{1,0:T(8,128)(2,1)}) custom-call(bf16[384,304]{1,0:T(8,128)(2,1)} %get-tuple-element.43.place, f32[2,2,112,384]{3,2,1,0:T(8,128)} %get-tuple-element.44.filt_l, f32[2,2,24,384]{3,2,1,0:T(8,128)} %get-tuple-element.45.filt_s, ...), custom_call_target="tpu_custom_call" | custom-call | tf_op jit(solution)/shard_map/backward/pallas_call | solution.py:672
  140.0 0.6 compare_select_fusion.order
  140.6 11.1 %unpack.1 = (f32[24,1,14,4,384]{4,3,2,1,0:T(4,128)}, f32[72,1,6,2,384]{4,3,2,1,0:T(2,128)}, f32[24,1,14,4,384]{4,3,2,1,0:T(4,128)}, f32[72,1,6,2,384]{4,3,2,1,0:...) custom-call(s32[4]{0:T(128)} %compare_select_fusion.order, ...), custom_call_target="tpu_custom_call" | custom-call | tf_op jit(solution)/shard_map/unpack/pallas_call | solution.py:779

commit v5 on v4

--- a/solution.py
+++ b/solution.py
@@ -25,31 +25,31 @@
 SMALL = 512
 PLAN = {
     (0, 0): [(-3, 0)],
-    (0, 9): [(0, 0), (-3, 1)],
-    (1, 2): [(0, 1), (-3, 2)],
-    (1, 9): [(1, 0)],
-    (2, 0): [(-3, 3)],
-    (2, 2): [(1, 1)],
-    (2, 9): [(2, 0), (-3, 4)],
-    (3, 0): [(0, 2)],
-    (3, 2): [(2, 1)],
-    (4, 0): [(-3, 5)],
-    (4, 2): [(1, 2)],
-    (5, 9): [(2, 2)],
-    (6, 0): [(0, 3)],
-    (6, 9): [(3, 0)],
-    (7, 0): [(1, 3)],
+    (0, 3): [(0, 0), (-3, 1)],
+    (1, 1): [(0, 1), (-3, 2)],
+    (1, 3): [(1, 0)],
+    (1, 9): [(-3, 3)],
+    (2, 1): [(1, 1)],
+    (2, 3): [(0, 2), (2, 0)],
+    (2, 9): [(-3, 4)],
+    (3, 1): [(2, 1)],
+    (3, 9): [(-3, 5)],
+    (4, 0): [(1, 2)],
+    (5, 2): [(0, 3), (2, 2)],
+    (6, 3): [(3, 0)],
+    (6, 9): [(1, 3)],
     (7, 1): [(3, 1)],
-    (7, 9): [(2, 3), (4, 0)],
-    (8, 2): [(4, 1)],
-    (8, 9): [(0, 4), (3, 2), (5, 0)],
-    (9, 2): [(5, 1), (1, 4)],
+    (7, 3): [(0, 4), (4, 0)],
+    (8, 1): [(4, 1)],
+    (8, 3): [(2, 3), (3, 2), (5, 0)],
+    (9, 1): [(5, 1)],
+    (9, 2): [(1, 4), (0, 5)],
     (9, 9): [(-2, 0)],
-    (10, 1): [(4, 2)],
-    (10, 9): [(2, 4)],
+    (10, 1): [(0, 6), (4, 2)],
     (11, 0): [(-2, 1)],
-    (11, 1): [(0, 5)],
-    (11, 9): [(-1, 0), (0, 6), (-2, 2), (3, 3), (5, 2), (-1, 1), (4, 3), (1, 5), (1, 6), (2, 5), (-1, 2), (-2, 3), (2, 6), (3, 4), (5, 3), (4, 4), (-2, 4), (3, 5), (3, 6), (-1, 3), (5, 4), (-2, 5), (4, 5), (4, 6), (-1, 4), (5, 5), (-1, 5), (5, 6), (-1, 6)],
+    (11, 1): [(2, 4)],
+    (11, 2): [(5, 2)],
+    (11, 9): [(-1, 0), (1, 5), (-1, 1), (3, 3), (1, 6), (2, 5), (-2, 2), (4, 3), (-1, 2), (2, 6), (5, 3), (3, 4), (-2, 3), (4, 4), (-2, 4), (-1, 3), (3, 5), (3, 6), (-2, 5), (5, 4), (4, 5), (4, 6), (-1, 4), (5, 5), (-1, 5), (5, 6), (-1, 6)],
 }
 MESH = pl.DeviceIdType.MESH
 VMEM_LIMIT = 60 * 2**20
@@ -393,7 +393,7 @@
         base, count = self.region(part, level + 1)
         rows = self.rows(base, count)
         return pltpu.make_async_remote_copy(
-            src_ref=self.full.at[rows], dst_ref=self.full.at[rows],
+            src_ref=self.full.at[rows], dst_ref=(self.full if level else self.out).at[rows],
             send_sem=self.sems[level].at[2, part], recv_sem=self.sems[level].at[3, part],
             device_id=self.others[level][step - 1][0], device_id_type=MESH)
 
@@ -402,7 +402,7 @@
         pltpu.make_async_copy(every, every, self.sems[level].at[sem, part]).wait()
 
     def save(self, part):
-        rows = self.rows(part * self.count, self.count)
+        rows = self.rows(*self.region(part, 1))
         return pltpu.make_async_copy(self.full.at[rows], self.out.at[rows], self.save_sem.at[part])
 
     def stage(self, part, k):
@@ -424,7 +424,7 @@
         if top <= k < 2 * top:
             for step in range(1, self.size[2 * top - 1 - k]):
                 self.up(part, 2 * top - 1 - k, step).start()
-        if k == 2 * top:
+        if k == 2 * top - 1:
             self.save(part).start()
 
 
@@ -455,7 +455,7 @@
 def backward_kernel(row_count, batch_count, groups, pair, place, filt_l, filt_s, gain1, gain2, w1, w2, tl, ts, tlb, tsb,
                     mix, fold, outs, do_in, xs, zs, both_scales, spec, vs, gs, ps,
                     out_land, grad_land, weights_out, small_out,
-                    dx, dv, do, dot_, vt, dh, gslots, dvec, dhid, dfl, dfs, out_sem, grad_sem, own_sem, *sums):
+                    dx, dv, do, dh, gslots, dvec, dhid, dfl, dfs, out_sem, grad_sem, own_sem, *sums):
     i = pl.program_id(0)
     batch, row = lax.axis_index("batch"), lax.axis_index("rows")
     chunks, pairs = FF // CB, groups // pair
@@ -543,30 +543,31 @@
             low = dx[g].astype(BF16)
             do[g] = low
             dvec[layer, 4:5] += jnp.sum(low.astype(F32), axis=0, keepdims=True)
-        dot_[...] = do[...].reshape(groups * T, D).T
-        vt[:D] = vs[0].reshape(groups * T, D).T
-        vt[D:] = jnp.ones((16, groups * T), BF16)
         dv[...] = jnp.zeros_like(dv)
 
     @pl.when((i < compute_steps) & (q < chunks))
     def _():
+        sums = jnp.zeros((1, CB), F32)
         for g in range(0, groups, pair):
             rows = slice(g * T, (g + pair) * T)
             some = do[g : g + pair].reshape(pair * T, D)
             slope = ps[0, g : g + pair].reshape(pair * T, CB)
             part = (dot_nt(some, w2[0]) * slope.astype(F32)).astype(BF16)
             dh[rows] = part
-            dv[g : g + pair] += dot_nt(part, w1[0]).reshape(pair, T, D)
+            sums = sums + jnp.sum(part.astype(F32), axis=0, keepdims=True)
             advance(g // pair, first_steps)
         part = (LAYERS - 1 - layer) * chunks + q
         base = part * part_rows
-        one = dot(vt[...], dh[...])
-        dhid[layer, :, pl.ds(pl.multiple_of(q * CB, CB), CB)] = one[D : D + 1]
-        two = dot(dot_[...], gs[0].reshape(groups * T, CB))
+        dhid[layer, :, pl.ds(pl.multiple_of(q * CB, CB), CB)] = sums
+        one = dot_tn(vs[0].reshape(groups * T, D), dh[...])
+        two = dot_tn(do[...].reshape(groups * T, D), gs[0].reshape(groups * T, CB))
         for c in range(CB // width):
             cols = slice(c * width, (c + 1) * width)
             weights.acc[weights.rows(base + c * D, D), :] = one[:D, cols].astype(BF16)
             weights.acc[weights.rows(base + (CB // width + c) * D, D), :] = two[:, cols].astype(BF16)
+        advance(3, first_steps)
+        for g in range(0, groups, pair):
+            dv[g : g + pair] += dot_nt(dh[g * T : (g + pair) * T], w1[0]).reshape(pair, T, D)
 
     @pl.when((i < compute_steps) & (q >= chunks))
     def _():
@@ -617,16 +618,23 @@
                 for m in range(row_count):
                     gslots[m, first + j] = spread[m * BAND : (m + 1) * BAND, j * D : (j + 1) * D]
 
-    @pl.when(i == compute_steps - 1)
-    def _():
-        small.acc[...] = jnp.zeros_like(small.acc)
+    def lay_out(layers):
         exact = partial(jnp.dot, preferred_element_type=F32, precision=HIGHEST)
         mix_t = mix[...].T
-        for n in range(LAYERS):
+        for n in layers:
             for c in range(2):
                 at = (n * 2 + c) * NL
                 small.acc[at : at + NL, :] = (dfl[n, c * NL : (c + 1) * NL] * fold[...]
                                               + exact(mix_t, dfs[n, c * NS : (c + 1) * NS])).astype(BF16)
+
+    @pl.when(i == compute_steps - pairs - 1)
+    def _():
+        small.acc[...] = jnp.zeros_like(small.acc)
+        lay_out(range(1, LAYERS))
+
+    @pl.when(i == compute_steps - 1)
+    def _():
+        lay_out([0])
         at = LAYERS * 2 * NL
         rest = [dvec[n, k : k + 1] for n in range(LAYERS) for k in range(5)]
         rest += [dhid[n, :, c : c + D] for n in range(LAYERS) for c in range(0, FF, D)]
@@ -680,7 +688,6 @@
         out_shape=[jax.ShapeDtypeStruct((rows, groups, BAND, D), BF16)] * 2
         + [jax.ShapeDtypeStruct((LAYERS * chunks * part_rows, width), BF16), jax.ShapeDtypeStruct((small_rows, D), BF16)],
         scratch_shapes=[pltpu.VMEM((groups, T, D), F32), pltpu.VMEM((groups, T, D), F32), pltpu.VMEM((groups, T, D), BF16),
-                        pltpu.VMEM((D, groups * T), BF16), pltpu.VMEM((D + 16, groups * T), BF16),
                         pltpu.VMEM((groups * T, CB), BF16), pltpu.VMEM((rows, groups, BAND, D), BF16),
                         pltpu.VMEM((LAYERS, 5, D), F32), pltpu.VMEM((LAYERS, 1, FF), F32),
                         pltpu.VMEM((LAYERS, 2 * NL, D), F32), pltpu.VMEM((LAYERS, 2 * NS, D), F32),

time: 152 us -> 152 us (level)
  no operation moved by 1% of the time
where the time goes in v5:
time: 152 us; the launch traced here: 151 us
  Pallas kernels  150 us (99%)
    pallas_call x1, Pallas kernels, backward(): pl.pallas_call(partial(backward_kernel, rows, batch, groups, pair), grid=...  92.4 us
    pallas_call x1, Pallas kernels, forward(): pl.pallas_call(partial(forward_kernel, rows, groups, pair), grid=(groups...  46.6 us
    pallas_call x1, Pallas kernels, unpack(): pl.pallas_call(partial(unpack_kernel, groups), in_specs=[scalars()] + [hb...  11.1 us

profile of v5, /device:TPU:0, one launch (start us, length us, event | category | flops | bytes accessed | tf_op | source)
XLA Modules:
  0.0 151.5 jit_solution(1737868680753900861)
XLA Ops:
  0.6 46.6 %forward.1 = (bf16[4,6,96,384]{3,2,1,0:T(8,128)(2,1)}, bf16[2,6,304,384]{3,2,1,0:T(8,128)(2,1)}, bf16[2,6,304,384]{3,2,1,0:T(8,128)(2,1)}, f32[2,6,304,2]{3,2,1,...) custom-call(bf16[24,1,14,4,384]{4,3,2,1,0:T(4,128)(2,1)} %bitcast.12, ...), custom_call_target="tpu_custom_call" | custom-call | tf_op jit(solution)/shard_map/forward/pallas_call | solution.py:315
  47.2 92.4 %backward.1 = (bf16[4,6,96,384]{3,2,1,0:T(8,128)(2,1)}, bf16[4,6,96,384]{3,2,1,0:T(8,128)(2,1)}, bf16[9216,256]{1,0:T(8,128)(2,1)}, bf16[512,384]{1,0:T(8,128)(2,1)}) custom-call(bf16[384,304]{1,0:T(8,128)(2,1)} %get-tuple-element.43.place, f32[2,2,112,384]{3,2,1,0:T(8,128)} %get-tuple-element.44.filt_l, f32[2,2,24,384]{3,2,1,0:T(8,128)} %get-tuple-element.45.filt_s, ...), custom_call_target="tpu_custom_call" | custom-call | tf_op jit(solution)/shard_map/backward/pallas_call | solution.py:680
  139.6 0.6 compare_select_fusion.order
  140.2 11.1 %unpack.1 = (f32[24,1,14,4,384]{4,3,2,1,0:T(4,128)}, f32[72,1,6,2,384]{4,3,2,1,0:T(2,128)}, f32[24,1,14,4,384]{4,3,2,1,0:T(4,128)}, f32[72,1,6,2,384]{4,3,2,1,0:...) custom-call(s32[4]{0:T(128)} %compare_select_fusion.order, ...), custom_call_target="tpu_custom_call" | custom-call | tf_op jit(solution)/shard_map/unpack/pallas_call | solution.py:786

commit v6 on v5

--- a/solution.py
+++ b/solution.py
@@ -49,7 +49,7 @@
     (11, 0): [(-2, 1)],
     (11, 1): [(2, 4)],
     (11, 2): [(5, 2)],
-    (11, 9): [(-1, 0), (1, 5), (-1, 1), (3, 3), (1, 6), (2, 5), (-2, 2), (4, 3), (-1, 2), (2, 6), (5, 3), (3, 4), (-2, 3), (4, 4), (-2, 4), (-1, 3), (3, 5), (3, 6), (-2, 5), (5, 4), (4, 5), (4, 6), (-1, 4), (5, 5), (-1, 5), (5, 6), (-1, 6)],
+    (11, 9): [(-1, 0), (1, 5), (-1, 1), (3, 3), (1, 6), (2, 5), (4, 3), (-1, 2), (2, 6), (5, 3), (-2, 2), (3, 4), (4, 4), (-2, 3), (-1, 3), (-2, 4), (3, 5), (3, 6), (5, 4), (-2, 5), (4, 5), (4, 6), (-1, 4), (5, 5), (-1, 5), (5, 6), (-1, 6)],
 }
 MESH = pl.DeviceIdType.MESH
 VMEM_LIMIT = 60 * 2**20

time: 152 us -> 151 us (level)
  no operation moved by 1% of the time
where the time goes in v6:
time: 151 us
  Pallas kernels  149 us (99%)
    pallas_call x1, Pallas kernels, backward(): pl.pallas_call(partial(backward_kernel, rows, batch, groups, pair), grid=...  91.6 us
    pallas_call x1, Pallas kernels, forward(): pl.pallas_call(partial(forward_kernel, rows, groups, pair), grid=(groups...  46.6 us
    pallas_call x1, Pallas kernels, unpack(): pl.pallas_call(partial(unpack_kernel, groups), in_specs=[scalars()] + [hb...  11.1 us

profile of v6, /device:TPU:0, one launch (start us, length us, event | category | flops | bytes accessed | tf_op | source)
XLA Modules:
  0.0 150.7 jit_solution(12294315811084168235)
XLA Ops:
  0.6 46.6 %forward.1 = (bf16[4,6,96,384]{3,2,1,0:T(8,128)(2,1)}, bf16[2,6,304,384]{3,2,1,0:T(8,128)(2,1)}, bf16[2,6,304,384]{3,2,1,0:T(8,128)(2,1)}, f32[2,6,304,2]{3,2,1,...) custom-call(bf16[24,1,14,4,384]{4,3,2,1,0:T(4,128)(2,1)} %bitcast.12, ...), custom_call_target="tpu_custom_call" | custom-call | tf_op jit(solution)/shard_map/forward/pallas_call | solution.py:315
  47.2 91.6 %backward.1 = (bf16[4,6,96,384]{3,2,1,0:T(8,128)(2,1)}, bf16[4,6,96,384]{3,2,1,0:T(8,128)(2,1)}, bf16[9216,256]{1,0:T(8,128)(2,1)}, bf16[512,384]{1,0:T(8,128)(2,1)}) custom-call(bf16[384,304]{1,0:T(8,128)(2,1)} %get-tuple-element.43.place, f32[2,2,112,384]{3,2,1,0:T(8,128)} %get-tuple-element.44.filt_l, f32[2,2,24,384]{3,2,1,0:T(8,128)} %get-tuple-element.45.filt_s, ...), custom_call_target="tpu_custom_call" | custom-call | tf_op jit(solution)/shard_map/backward/pallas_call | solution.py:680
  138.8 0.6 compare_select_fusion.order
  139.4 11.1 %unpack.1 = (f32[24,1,14,4,384]{4,3,2,1,0:T(4,128)}, f32[72,1,6,2,384]{4,3,2,1,0:T(2,128)}, f32[24,1,14,4,384]{4,3,2,1,0:T(4,128)}, f32[72,1,6,2,384]{4,3,2,1,0:...) custom-call(s32[4]{0:T(128)} %compare_select_fusion.order, ...), custom_call_target="tpu_custom_call" | custom-call | tf_op jit(solution)/shard_map/unpack/pallas_call | solution.py:786
